TPU v7x, 32 devices: a whole 2x2x4 slice. The times are simulated.
32 devices in a mesh: groups: 2 (over y), band: 4 (over z), sub: 2 (over x), cfg: 2 (over core).
Axes of the slice: x: 2, y: 2, z: 4, core: 2. Of those that a mesh axis runs over, the one named last changes fastest.
Arguments:
- latents: float32 [32, 32, 256], P('groups', 'band', 'sub'), parts along dimension 0, may hold values from -6 to 6
- in_weight: bfloat16 [3, 3, 16, 320], replicated, may hold values from -0.5 to 0.5
- mid_weight: bfloat16 [3, 3, 320, 320], replicated, may hold values from -0.109375 to 0.109375
- out_weight: bfloat16 [3, 3, 16, 320], replicated, may hold values from -0.109375 to 0.109375
- norm_mean: float32 [2, 320], replicated, may hold values from -3 to 3
- norm_rstd: float32 [2, 320], replicated, may hold values from 0.5 to 2
- cond_embed: float32 [2, 640], P('cfg', 'groups'), parts along dimension 1, may hold values from -6 to 6
- time_embed: float32 [1000, 320], replicated, may hold values from -6 to 6
- time_index: int32 [2], replicated, may hold values from 0 to 999
- coef_index: int32 [2], replicated, may hold values from 0 to 999
- sampler_table: float32 [3, 1000], replicated, may hold values from -0.4 to 4, as said below
Outputs:
- denoised: float32 [32, 32, 256], P('groups', 'band', 'sub'), parts along dimension 0
There are 2 independent parts, one for each index of `groups`. A program takes and returns all parts, laid end to end along the dimension named above; an argument that names none is the same for every part. Nothing has to cross between parts.
Inputs may be any that keep to these rules, and one draw needn't show every extreme that they name: `sampler_table`: column k holds one sampler step: row 0 scales the latent (0.8 to 1.2), row 1 scales the guided noise (-0.4 to -0.1), row 2 is the guidance scale (1.5 to 4.0).
All inputs are finite; a program needn't handle non-finite values.
Results may differ from a plain program's by a relative error of at most 0.013.
Values may be sent and summed in bfloat16 or wider, within the bound.
A program may use at most 64 MiB of HBM per device.

v0:
```python
import jax
import jax.numpy as jnp
from jax import lax
from jax.sharding import PartitionSpec as P


def padded(cells, sides, width):
    for axis, dim in sides:
        count = lax.axis_size(axis)
        ends = count - 1
        head = lax.slice_in_dim(cells, 0, width, axis=dim)
        tail = lax.slice_in_dim(cells, cells.shape[dim] - width, cells.shape[dim], axis=dim)
        cells = jnp.concatenate(
            [
                lax.ppermute(tail, axis, [(i, (i + 1) % count) for i in range(ends)]),
                cells,
                lax.ppermute(head, axis, [((i + 1) % count, i) for i in range(ends)]),
            ],
            axis=dim,
        )
    return cells


def partner(block, axis, stride):
    count = lax.axis_size(axis)
    route = []
    for low in range(count):
        high = low | 1 << stride
        if high != low and high < count:
            route += [(low, high), (high, low)]
    return lax.ppermute(block, axis, route)


def conv_valid(source, kernel, pattern):
    out_rows = source.shape[1] - 2
    out_cols = source.shape[2] - 2
    chans = source.shape[0]
    stacked = jnp.concatenate(
        [source[:, :, tap_col : tap_col + out_cols] for tap_col in range(3)], axis=0
    )
    total = None
    for tap_row in range(3):
        taps = kernel[tap_row]
        if pattern == "co,chw->ohw":
            matrix = taps.reshape(3 * chans, taps.shape[2])
        else:
            matrix = jnp.transpose(taps, (1, 0, 2)).reshape(taps.shape[1], 3 * chans)
        window = stacked[:, tap_row : tap_row + out_rows, :]
        product = jnp.einsum(pattern, matrix, window, preferred_element_type=jnp.float32)
        total = product if total is None else total + product
    return total


def activate(field, centre, spread):
    return jax.nn.silu((field - centre[:, None, None]) * spread[:, None, None]).astype(jnp.bfloat16)


def region_mask(row_count, col_count, margin):
    row_start = lax.axis_index("band") * row_count - margin
    col_start = lax.axis_index("sub") * col_count - margin
    height = row_count * lax.axis_size("band")
    width = col_count * lax.axis_size("sub")
    row_place = row_start + jnp.arange(row_count + 2 * margin, dtype=jnp.int32)
    col_place = col_start + jnp.arange(col_count + 2 * margin, dtype=jnp.int32)
    row_inside = (row_place >= 0) & (row_place < height)
    col_inside = (col_place >= 0) & (col_place < width)
    return (row_inside[:, None] & col_inside[None, :]).astype(jnp.bfloat16)


def noise_region(source, inside, kernels, offset):
    in_weight, mid_weight, out_weight, norm_mean, norm_rstd = kernels
    first_map = conv_valid(source * inside, in_weight, "co,chw->ohw") + offset[:, None, None]
    lifted = activate(first_map, norm_mean[0], norm_rstd[0]) * inside[1:-1, 1:-1]
    second = first_map[:, 1:-1, 1:-1] + conv_valid(lifted, mid_weight, "oc,chw->ohw")
    lowered = activate(second, norm_mean[1], norm_rstd[1]) * inside[2:-2, 2:-2]
    return conv_valid(lowered, out_weight, "oc,chw->ohw")


def shards(
    latents,
    in_weight,
    mid_weight,
    out_weight,
    norm_mean,
    norm_rstd,
    cond_embed,
    time_embed,
    time_index,
    coef_index,
    sampler_table,
):
    kernels = (in_weight, mid_weight, out_weight, norm_mean, norm_rstd)
    row_count = latents.shape[1]
    col_count = latents.shape[2]
    sample_steps = time_index.shape[0]
    margin = 0
    margin = 3 * sample_steps
    current = padded(latents.astype(jnp.bfloat16), (("band", 1), ("sub", 2)), margin).astype(
        latents.dtype
    )
    is_plain = lax.axis_index("cfg") == 0
    for sample_step in range(sample_steps):
        time_row = lax.dynamic_index_in_dim(time_embed, time_index[sample_step], 0, keepdims=False)
        sampler_col = lax.dynamic_index_in_dim(
            sampler_table, coef_index[sample_step], 1, keepdims=False
        )
        offset = time_row + cond_embed[0]
        source = current.astype(jnp.bfloat16)
        own_noise = noise_region(source, region_mask(row_count, col_count, margin), kernels, offset)
        kept_state = current[:, 3:-3, 3:-3]
        margin = margin - 3
        other_noise = partner(own_noise.astype(jnp.bfloat16), "cfg", 0).astype(own_noise.dtype)
        plain_noise = jnp.where(is_plain, own_noise, other_noise)
        steered_noise = jnp.where(is_plain, other_noise, own_noise)
        guided = plain_noise + sampler_col[2] * (steered_noise - plain_noise)
        current = sampler_col[0] * kept_state + sampler_col[1] * guided
    return current


def solution(mesh):
    return jax.shard_map(
        shards,
        mesh=mesh,
        in_specs=(
            P("groups", "band", "sub"),
            P(),
            P(),
            P(),
            P(),
            P(),
            P("cfg", "groups"),
            P(),
            P(),
            P(),
            P(),
        ),
        out_specs=P("groups", "band", "sub"),
        check_vma=False,
    )
```

profile of v0, /device:TPU:0, one launch (start us, length us, event | category | flops | bytes accessed | tf_op | source)
XLA Modules:
  0.0 75.2 jit_solution(12962714355486491412)
XLA Ops:
  0.0 0.9 %copy.60 = bf16[16,8,128]{2,0,1:T(8,128)(2,1)S(1)} copy(f32[16,8,128]{2,1,0:T(8,128)} %param.11) | data formatting | bytes 98304 | tf_op args[0]
  0.9 0.0 copy-start.3
  0.9 0.0 copy-start.4
  0.9 4.9 %collective-permute-start = (bf16[16,6,128]{2,0,1:T(8,128)(2,1)S(1)}, bf16[16,6,128]{2,0,1:T(8,128)(2,1)S(1)}, u32[]{:S(2)}, u32[]{:S(2)}) collective-permute-start(bf16[16,6,128]{2,0,1:T(8,128)(2,1)S(1)} %get-tuple-element.44), channel_id=1, source_target_pairs={{0,4},{4,8},{8,12},{1,5},{5,9},{9,13},{2,6},{6,10},{10,14},{3,7},{... | collective-permute-start | bytes 73736 | tf_op jit(solution)/shard_map/ppermute | solution.py:15
  5.9 1.3 %collective-permute-start.1 = (bf16[16,6,128]{2,0,1:T(8,128)(2,1)S(1)}, bf16[16,6,128]{2,0,1:T(8,128)(2,1)S(1)}, u32[]{:S(2)}, u32[]{:S(2)}) collective-permute-start(bf16[16,6,128]{2,0,1:T(8,128)(2,1)S(1)} %get-tuple-element.45), channel_id=1, source_target_pairs={{4,0},{8,4},{12,8},{5,1},{9,5},{13,9},{6,2},{10,6},{14,10},{7,3},{... | collective-permute-start | bytes 73736 | tf_op jit(solution)/shard_map/ppermute | solution.py:17
  7.2 1.4 %fusion.43 = (s32[1]{0:T(128)}, s32[1]{0:T(128)}) fusion(s32[2]{0:T(128)} %param.19), kind=kLoop, calls=%fused_computation.90 | loop fusion | bytes 16 | tf_op jit(solution)/shard_map/slice | solution.py:103
  11.1 0.8 %fusion.37 = (bf16[1,3,16,320]{3,2,1,0:T(8,128)(2,1)S(1)}, bf16[1,3,16,320]{3,2,1,0:T(8,128)(2,1)S(1)}, bf16[1,3,16,320]{3,2,1,0:T(8,128)(2,1)S(1)}) fusion(bf16[3,3,16,320]{3,2,1,0:T(8,128)(2,1)} %param.12), kind=kLoop, calls=%fused_computation.84 | loop fusion | bytes 184320 | tf_op jit(solution)/shard_map/slice | solution.py:43
  12.0 0.8 %copy.26 = f32[1,320]{0,1:T(8,128)S(1)} copy(f32[1,320]{1,0:T(1,128)} %param.17) | data formatting | bytes 2560 | tf_op args[6]
  12.8 0.0 copy-start.11
  12.8 1.8 %slice_bitcast_fusion.1 = (bf16[320,3,320]{2,0,1:T(8,128)(2,1)S(1)}, bf16[320,3,320]{2,0,1:T(8,128)(2,1)S(1)}, bf16[320,3,320]{2,0,1:T(8,128)(2,1)S(1)}) fusion(bf16[3,3,320,320]{3,2,1,0:T(8,128)(2,1)} %param.13), kind=kLoop, calls=%fused_computation.27 | loop fusion | bytes 3686400 | tf_op jit(solution)/shard_map/transpose | solution.py:47
  14.7 0.1 and_convert_fusion
  16.0 0.6 slice_reduce_fusion
  16.6 0.1 and_convert_fusion.1
  16.7 1.9 %add_reduce_fusion = (f32[320]{0:T(512)}, f32[320]{0:T(512)}) fusion(f32[1,320]{0,1:T(8,128)S(1)} %copy.26, f32[1000,320]{0,1:T(8,128)} %param.18, s32[]{:T(128)S(6)} %select_n.45, s32[]{:T(128)S(6)} %select_n.41), kind=kLoop, calls=%fused_computation.39 | loop fusion | flops 640 | bytes 6408 | tf_op jit(solution)/shard_map/add | solution.py:107
  18.6 0.6 fusion.42
  23.0 0.7 fusion.38
  23.8 3.4 %collective-permute-start.2 = (bf16[16,20,6]{2,0,1:T(8,128)(2,1)}, bf16[16,20,6]{2,0,1:T(8,128)(2,1)S(1)}, u32[]{:S(2)}, u32[]{:S(2)}) collective-permute-start(bf16[16,20,6]{2,0,1:T(8,128)(2,1)} %get-tuple-element.42), channel_id=1, source_target_pairs={{0,2},{1,3},{4,6},{5,7},{8,10},{9,11},{12,14},{13,15},{16,18},{17,... | collective-permute-start | bytes 11528 | tf_op jit(solution)/shard_map/ppermute | solution.py:15
  27.2 1.3 %collective-permute-start.3 = (bf16[16,20,6]{2,0,1:T(8,128)(2,1)S(1)}, bf16[16,20,6]{2,0,1:T(8,128)(2,1)S(1)}, u32[]{:S(2)}, u32[]{:S(2)}) collective-permute-start(bf16[16,20,6]{2,0,1:T(8,128)(2,1)S(1)} %get-tuple-element.43), channel_id=1, source_target_pairs={{2,0},{3,1},{6,4},{7,5},{10,8},{11,9},{14,12},{15,13},{18,16},{19,... | collective-permute-start | bytes 11528 | tf_op jit(solution)/shard_map/ppermute | solution.py:17
  28.5 1.4 %constant_dynamic-slice_fusion.1 = (f32[3,1]{1,0:T(4,128)}, f32[3,1]{1,0:T(4,128)}) fusion(f32[3,1000]{1,0:T(4,128)} %param.21, s32[]{:T(128)S(6)} %select_n.38, s32[]{:T(128)S(6)} %select_n.39), kind=kLoop, calls=%fused_computation.67 | loop fusion | bytes 56 | tf_op jit(solution)/shard_map/jit(dynamic_index_in_dim)/dynamic_slice | solution.py:104
  29.8 0.1 slice.316
  29.9 0.1 slice.320
  30.0 0.1 slice.329
  30.0 0.1 slice.333
  30.1 0.4 copy.29
  30.5 0.4 copy.27
  30.9 0.4 copy.31
  31.3 0.1 reshape.160
  31.4 0.1 reshape.161
  31.5 0.1 reshape.162
  31.7 1.8 %collective-permute-done.3 = bf16[16,20,6]{2,0,1:T(8,128)(2,1)S(1)} collective-permute-done((bf16[16,20,6]{2,0,1:T(8,128)(2,1)S(1)}, bf16[16,20,6]{2,0,1:T(8,128)(2,1)S(1)}, u32[]{:S(2)}, u32[]{:S(2)}) %collective-permute-start.3) | collective-permute-done | bytes 3872 | tf_op jit(solution)/shard_map/ppermute | solution.py:17
  33.5 0.2 broadcast_multiply_fusion
  33.7 0.2 fusion.35
  33.8 0.7 fusion.22
  34.6 0.7 fusion.23
  35.3 1.8 %fusion.4 = (bf16[320,18,138]{0,2,1:T(8,128)(2,1)S(1)}, f32[320,18,138]{0,2,1:T(8,128)S(1)}) fusion(f32[320]{0:T(512)S(1)} %copy-done.9, f32[320]{0:T(512)S(1)} %copy-done.10, bf16[18,138]{1,0:T(8,128)(2,1)S(1)} %slice.316, f32[320]{0:T(512)S(1)} %copy-done.6, bf16[48,320,1]{1,0,2:T(8,128)(2,1)S(1)} %bitcast.103, ...), kind=kOutput, calls=%fused_computation.16 | convolution fusion | flops 85847040 | bytes 11432808 | tf_op jit(solution)/shard_map/co,chw->ohw/dot_general | solution.py:49
  37.1 1.1 %fusion.31 = (bf16[320,18,136]{0,2,1:T(8,128)(2,1)S(1)}, bf16[320,18,136]{0,2,1:T(8,128)(2,1)S(1)}, bf16[320,18,136]{0,2,1:T(8,128)(2,1)S(1)}) fusion(bf16[320,18,138]{0,2,1:T(8,128)(2,1)S(1)} %get-tuple-element.58), kind=kLoop, calls=%fused_computation.78 | loop fusion | bytes 9400320 | tf_op jit(solution)/shard_map/slice | solution.py:39
  38.2 2.6 %fusion.28 = f32[16,136,320]{2,1,0:T(8,128)S(1)} fusion(bf16[320,960,1]{0,1,2:T(8,128)(2,1)S(1)} %bitcast.95, bf16[320,18,136]{0,2,1:T(8,128)(2,1)S(1)} %get-tuple-element.19, bf16[320,18,136]{0,2,1:T(8,128)(2,1)S(1)} %get-tuple-element.20, bf16[320,18,136]{0,2,1:T(8,128)(2,1)S(1)} %get-tuple-element.18), kind=kOutput, calls=%fused_computation.76 | convolution fusion | flops 1351034880 | bytes 8099840 | tf_op jit(solution)/shard_map/oc,chw->ohw/dot_general | solution.py:49
  40.8 0.0 copy-start.7
  40.8 2.6 %fusion.29 = f32[16,136,320]{2,1,0:T(8,128)S(1)} fusion(bf16[320,960,1]{0,1,2:T(8,128)(2,1)S(1)} %bitcast.97, bf16[320,18,136]{0,2,1:T(8,128)(2,1)S(1)} %get-tuple-element.19, bf16[320,18,136]{0,2,1:T(8,128)(2,1)S(1)} %get-tuple-element.20, bf16[320,18,136]{0,2,1:T(8,128)(2,1)S(1)} %get-tuple-element.18), kind=kOutput, calls=%fused_computation.77 | convolution fusion | flops 1351034880 | bytes 8099840 | tf_op jit(solution)/shard_map/oc,chw->ohw/dot_general | solution.py:49
  43.4 4.6 %fusion.5 = bf16[320,16,136]{0,2,1:T(8,128)(2,1)S(1)} fusion(f32[320]{0:T(512)S(1)} %copy-done.7, f32[320]{0:T(512)S(1)} %copy-done.8, bf16[320,960,1]{0,1,2:T(8,128)(2,1)S(1)} %bitcast.93, f32[16,136,320]{2,1,0:T(8,128)S(1)} %fusion.29, f32[16,136,320]{2,1,0:T(8,128)S(1)} %fusion.28, f32[320,18,138]{0,2,1:T(8,128)S(1)} %get-tuple-element.59, ...), kind=kOutput, calls=%fused_computation.17 | convolution fusion | flops 1358694400 | bytes 15069952 | tf_op jit(solution)/shard_map/oc,chw->ohw/dot_general | solution.py:49
  48.1 0.9 %fusion.32 = (bf16[320,16,134]{0,2,1:T(8,128)(2,1)S(1)}, bf16[320,16,134]{0,2,1:T(8,128)(2,1)S(1)}, bf16[320,16,134]{0,2,1:T(8,128)(2,1)S(1)}) fusion(bf16[320,16,136]{0,2,1:T(8,128)(2,1)S(1)} %fusion.5), kind=kLoop, calls=%fused_computation.79 | loop fusion | bytes 8232960 | tf_op jit(solution)/shard_map/slice | solution.py:39
  49.0 2.5 %fusion.27 = f32[14,134,16]{1,2,0:T(8,128)S(1)} fusion(bf16[16,960,1]{1,0,2:T(8,128)(2,1)S(1)} %reshape.160, bf16[320,16,134]{0,2,1:T(8,128)(2,1)S(1)} %get-tuple-element.22, bf16[320,16,134]{0,2,1:T(8,128)(2,1)S(1)} %get-tuple-element.23, bf16[320,16,134]{0,2,1:T(8,128)(2,1)S(1)} %get-tuple-element.21), kind=kOutput, calls=%fused_computation.75 | convolution fusion | flops 69980160 | bytes 4267264 | tf_op jit(solution)/shard_map/oc,chw->ohw/dot_general | solution.py:49
  51.5 2.5 %convolution_add_fusion.1 = f32[14,134,16]{1,2,0:T(8,128)S(1)} fusion(f32[14,134,16]{1,2,0:T(8,128)S(1)} %fusion.27, bf16[16,960,1]{1,0,2:T(8,128)(2,1)S(1)} %reshape.161, bf16[320,16,134]{0,2,1:T(8,128)(2,1)S(1)} %get-tuple-element.22, bf16[320,16,134]{0,2,1:T(8,128)(2,1)S(1)} %get-tuple-element.23, bf16[320,16,134]{0,2,1:T(8,128)(2,1)S(1)} %get-tuple-element.21), kind=kOutput, calls=%fused_computation.22 | convolution fusion | flops 70010176 | bytes 4387328 | tf_op jit(solution)/shard_map/oc,chw->ohw/dot_general | solution.py:49
  54.0 1.6 %fusion.44 = (bf16[16,14,134]{2,0,1:T(8,128)(2,1)S(1)}, f32[16,14,134]{2,0,1:T(8,128)S(1)}) fusion(f32[14,134,16]{1,2,0:T(8,128)S(1)} %convolution_add_fusion.1, bf16[16,960,1]{1,0,2:T(8,128)(2,1)S(1)} %reshape.162, bf16[320,16,134]{0,2,1:T(8,128)(2,1)S(1)} %get-tuple-element.22, bf16[320,16,134]{0,2,1:T(8,128)(2,1)S(1)} %get-tuple-element.23, ...), kind=kOutput, calls=%fused_computation.91 | convolution fusion | flops 70040192 | bytes 4447360 | tf_op jit(solution)/shard_map/oc,chw->ohw/dot_general | solution.py:49
  55.6 0.0 collective-permute-start.4
  55.7 0.6 fusion.40
  56.3 0.7 collective-permute-done.4
  57.0 2.1 %convert_multiply_fusion = (bf16[16,14,134]{2,0,1:T(8,128)(2,1)S(1)}, f32[16,14,134]{2,0,1:T(8,128)S(1)}) fusion(bf16[14,134]{1,0:T(8,128)(2,1)S(1)} %and_convert_fusion.1, f32[16,14,134]{2,0,1:T(8,128)S(1)} %get-tuple-element.61, f32[]{:T(128)} %bitcast.33, bf16[16,14,134]{2,0,1:T(8,128)(2,1)S(1)} %collective-permute-done.4, pred[]{:T(512)S(6)} %eq.3, ...), kind=kLoop, calls=%fused_computation.41 | loop fusion | flops 360192 | bytes 423989 | tf_op jit(solution)/shard_map/mul | solution.py:72
  59.0 0.1 fusion.36
  59.2 0.6 fusion.20
  59.8 0.6 fusion.21
  60.4 1.3 %fusion.6 = (bf16[320,12,132]{0,2,1:T(8,128)(2,1)S(1)}, f32[320,12,132]{0,2,1:T(8,128)S(1)}) fusion(f32[320]{0:T(512)S(1)} %copy-done.9, f32[320]{0:T(512)S(1)} %copy-done.10, bf16[12,132]{1,0:T(8,128)(2,1)S(1)} %slice.329, f32[320]{0:T(512)S(1)} %copy-done.5, bf16[48,320,1]{1,0,2:T(8,128)(2,1)S(1)} %bitcast.104, ...), kind=kOutput, calls=%fused_computation.18 | convolution fusion | flops 54768384 | bytes 7311456 | tf_op jit(solution)/shard_map/co,chw->ohw/dot_general | solution.py:49
  61.7 0.6 fusion.33
  62.4 1.6 %fusion.25 = f32[10,130,320]{2,1,0:T(8,128)S(1)} fusion(bf16[320,960,1]{0,1,2:T(8,128)(2,1)S(1)} %bitcast.96, bf16[320,12,130]{0,2,1:T(8,128)(2,1)S(1)} %get-tuple-element.25, bf16[320,12,130]{0,2,1:T(8,128)(2,1)S(1)} %get-tuple-element.26, bf16[320,12,130]{0,2,1:T(8,128)(2,1)S(1)} %get-tuple-element.24), kind=kOutput, calls=%fused_computation.73 | convolution fusion | flops 807705600 | bytes 5273600 | tf_op jit(solution)/shard_map/oc,chw->ohw/dot_general | solution.py:49
  64.0 1.7 %fusion.26 = f32[10,130,320]{2,1,0:T(8,128)S(1)} fusion(bf16[320,960,1]{0,1,2:T(8,128)(2,1)S(1)} %bitcast.98, bf16[320,12,130]{0,2,1:T(8,128)(2,1)S(1)} %get-tuple-element.25, bf16[320,12,130]{0,2,1:T(8,128)(2,1)S(1)} %get-tuple-element.26, bf16[320,12,130]{0,2,1:T(8,128)(2,1)S(1)} %get-tuple-element.24), kind=kOutput, calls=%fused_computation.74 | convolution fusion | flops 807705600 | bytes 5273600 | tf_op jit(solution)/shard_map/oc,chw->ohw/dot_general | solution.py:49
  65.7 3.0 %fusion.7 = bf16[320,10,130]{0,2,1:T(8,128)(2,1)S(1)} fusion(bf16[320,960,1]{0,1,2:T(8,128)(2,1)S(1)} %bitcast.94, f32[10,130,320]{2,1,0:T(8,128)S(1)} %fusion.26, f32[10,130,320]{2,1,0:T(8,128)S(1)} %fusion.25, f32[320,12,132]{0,2,1:T(8,128)S(1)} %get-tuple-element.63, f32[320]{0:T(512)S(1)} %copy-done.7, f32[320]{0:T(512)S(1)} %copy-done.8, ...), kind=kOutput, calls=%fused_computation.19 | convolution fusion | flops 812281600 | bytes 9438760 | tf_op jit(solution)/shard_map/oc,chw->ohw/dot_general | solution.py:49
  68.7 0.6 fusion.34
  69.3 0.7 fusion.24
  69.9 0.7 convolution_add_fusion.3
  70.6 0.7 fusion.45
  71.3 0.2 collective-permute-start.5
  71.5 1.1 %collective-permute-done.5 = bf16[16,8,128]{2,0,1:T(8,128)(2,1)S(1)} collective-permute-done((bf16[16,8,128]{2,0,1:T(8,128)(2,1)S(1)}, bf16[16,8,128]{2,0,1:T(8,128)(2,1)S(1)}, u32[]{:S(2)}, u32[]{:S(2)}) %collective-permute-start.5) | collective-permute-done | bytes 32800 | tf_op jit(solution)/shard_map/ppermute | solution.py:31
  72.6 2.0 %fusion.19 = f32[16,8,128]{2,0,1:T(8,128)S(1)} fusion(f32[16,8,128]{2,0,1:T(8,128)S(1)} %get-tuple-element.65, bf16[16,8,128]{2,0,1:T(8,128)(2,1)S(1)} %collective-permute-done.5, f32[16,14,134]{2,0,1:T(8,128)S(1)} %get-tuple-element.12, f32[]{:T(128)} %bitcast.45, f32[]{:T(128)} %bitcast.34, f32[]{:T(128)} %bitcast.1, pred[]{:T(512)S(6)} %eq.3), kind=kLoop, calls=%fused_computation.50 | loop fusion | flops 147456 | bytes 229389 | tf_op jit(solution)/shard_map/add | solution.py:116
  74.5 0.7 copy.43
  (33 shorter events, 0.2 us)
Async XLA Ops:
  0.0 14.6 %copy-start = (bf16[3,3,16,320]{3,2,1,0:T(8,128)(2,1)S(1)}, bf16[3,3,16,320]{3,2,1,0:T(8,128)(2,1)}, u32[]{:S(2)}) copy-start(bf16[3,3,16,320]{3,2,1,0:T(8,128)(2,1)} %param.14) | copy-start | bytes 276484
  0.9 15.1 %copy-start.3 = (f32[2,320]{1,0:T(2,128)S(1)}, f32[2,320]{1,0:T(2,128)}, u32[]{:S(2)}) copy-start(f32[2,320]{1,0:T(2,128)} %param.16) | copy-start | bytes 7684
  0.9 15.1 %copy-start.4 = (f32[2,320]{1,0:T(2,128)S(1)}, f32[2,320]{1,0:T(2,128)}, u32[]{:S(2)}) copy-start(f32[2,320]{1,0:T(2,128)} %param.15) | copy-start | bytes 7684
  0.9 22.1 %collective-permute-start = (bf16[16,6,128]{2,0,1:T(8,128)(2,1)S(1)}, bf16[16,6,128]{2,0,1:T(8,128)(2,1)S(1)}, u32[]{:S(2)}, u32[]{:S(2)}) collective-permute-start(bf16[16,6,128]{2,0,1:T(8,128)(2,1)S(1)} %get-tuple-element.44), channel_id=1, source_target_pairs={{0,4},{4,8},{8,12},{1,5},{5,9},{9,13},{2,6},{6,10},{10,14},{3,7},{... | collective-permute-start | bytes 73736 | tf_op jit(solution)/shard_map/ppermute | solution.py:15
  5.9 17.1 %collective-permute-start.1 = (bf16[16,6,128]{2,0,1:T(8,128)(2,1)S(1)}, bf16[16,6,128]{2,0,1:T(8,128)(2,1)S(1)}, u32[]{:S(2)}, u32[]{:S(2)}) collective-permute-start(bf16[16,6,128]{2,0,1:T(8,128)(2,1)S(1)} %get-tuple-element.45), channel_id=1, source_target_pairs={{4,0},{8,4},{12,8},{5,1},{9,5},{13,9},{6,2},{10,6},{14,10},{7,3},{... | collective-permute-start | bytes 73736 | tf_op jit(solution)/shard_map/ppermute | solution.py:17
  12.8 5.8 %copy-start.11 = (s32[2]{0:T(128)S(1)}, s32[2]{0:T(128)}, u32[]{:S(2)}) copy-start(s32[2]{0:T(128)} %param.20) | copy-start | bytes 28
  23.8 7.9 %collective-permute-start.2 = (bf16[16,20,6]{2,0,1:T(8,128)(2,1)}, bf16[16,20,6]{2,0,1:T(8,128)(2,1)S(1)}, u32[]{:S(2)}, u32[]{:S(2)}) collective-permute-start(bf16[16,20,6]{2,0,1:T(8,128)(2,1)} %get-tuple-element.42), channel_id=1, source_target_pairs={{0,2},{1,3},{4,6},{5,7},{8,10},{9,11},{12,14},{13,15},{16,18},{17,... | collective-permute-start | bytes 11528 | tf_op jit(solution)/shard_map/ppermute | solution.py:15
  27.2 6.3 %collective-permute-start.3 = (bf16[16,20,6]{2,0,1:T(8,128)(2,1)S(1)}, bf16[16,20,6]{2,0,1:T(8,128)(2,1)S(1)}, u32[]{:S(2)}, u32[]{:S(2)}) collective-permute-start(bf16[16,20,6]{2,0,1:T(8,128)(2,1)S(1)} %get-tuple-element.43), channel_id=1, source_target_pairs={{2,0},{3,1},{6,4},{7,5},{10,8},{11,9},{14,12},{15,13},{18,16},{19,... | collective-permute-start | bytes 11528 | tf_op jit(solution)/shard_map/ppermute | solution.py:17
  34.5 0.7 copy-start.6
  34.5 0.7 copy-start.9
  34.6 0.7 copy-start.10
  40.8 2.6 %copy-start.7 = (f32[320]{0:T(512)S(1)}, f32[320]{0:T(512)}, u32[]{:S(2)}) copy-start(f32[320]{0:T(512)} %get-tuple-element.9) | copy-start | bytes 3844
  40.8 2.6 %copy-start.8 = (f32[320]{0:T(512)S(1)}, f32[320]{0:T(512)}, u32[]{:S(2)}) copy-start(f32[320]{0:T(512)} %get-tuple-element.69) | copy-start | bytes 3844
  54.0 1.6 %copy-start.1 = (f32[3,1]{1,0:T(4,128)S(1)}, f32[3,1]{1,0:T(4,128)}, u32[]{:S(2)}) copy-start(f32[3,1]{1,0:T(4,128)} %get-tuple-element.46) | copy-start | bytes 40
  54.0 1.7 %copy-start.2 = (f32[3,1]{1,0:T(4,128)S(1)}, f32[3,1]{1,0:T(4,128)}, u32[]{:S(2)}) copy-start(f32[3,1]{1,0:T(4,128)} %get-tuple-element.47) | copy-start | bytes 40
  55.6 1.3 %collective-permute-start.4 = (bf16[16,14,134]{2,0,1:T(8,128)(2,1)S(1)}, bf16[16,14,134]{2,0,1:T(8,128)(2,1)S(1)}, u32[]{:S(2)}, u32[]{:S(2)}) collective-permute-start(bf16[16,14,134]{2,0,1:T(8,128)(2,1)S(1)} %get-tuple-element.60), channel_id=1, source_target_pairs={{0,1},{1,0},{2,3},{3,2},{4,5},{5,4},{6,7},{7,6},{8,9},{9,8},{10,11... | collective-permute-start | bytes 180104 | tf_op jit(solution)/shard_map/ppermute | solution.py:31
  59.2 1.3 %copy-start.5 = (f32[320]{0:T(512)S(1)}, f32[320]{0:T(512)}, u32[]{:S(2)}) copy-start(f32[320]{0:T(512)} %get-tuple-element.5) | copy-start | bytes 3844
  71.3 1.2 %collective-permute-start.5 = (bf16[16,8,128]{2,0,1:T(8,128)(2,1)S(1)}, bf16[16,8,128]{2,0,1:T(8,128)(2,1)S(1)}, u32[]{:S(2)}, u32[]{:S(2)}) collective-permute-start(bf16[16,8,128]{2,0,1:T(8,128)(2,1)S(1)} %get-tuple-element.64), channel_id=1, source_target_pairs={{0,1},{1,0},{2,3},{3,2},{4,5},{5,4},{6,7},{7,6},{8,9},{9,8},{10,11... | collective-permute-start | bytes 98312 | tf_op jit(solution)/shard_map/ppermute | solution.py:31
where the time goes:
time: 75.8 us; the launch traced here: 75.2 us
  matrix products  30.5 us (40%)
  local copies, waits for them, and re-layouts  15.7 us (21%)
  starting transfers between devices  11.1 us (15%)
  between operations  8.04 us (11%)
  other arithmetic  6.27 us (8%)
  waiting for transfers between devices  3.59 us (5%)
    dot_general x18, matrix products, conv_valid(): jnp.einsum(pattern, matrix, window, preferred_element_type=jnp.float32)  30.5 us
    ppermute x2, starting transfers between devices, padded(): lax.ppermute(tail, axis, [(i, (i + 1) % count) for i in range(ends)])  8.32 us
    slice x6, local copies, waits for them, and re-layouts, conv_valid(): source[:, :, tap_col:tap_col + out_cols]  3.52 us
    transpose x8, local copies, waits for them, and re-layouts, conv_valid(): matrix = jnp.transpose(taps, (1, 0, 2)).reshape(taps.shape[1], 3 * chans)  3 us
    ppermute x2, starting transfers between devices, padded(): lax.ppermute(head, axis, [((i + 1) % count, i) for i in range(ends)])  2.58 us
    mul x2, other arithmetic, noise_region(): source * inside  2.22 us
    add x1, other arithmetic, shards(): current = sampler_col[0] * kept_state + sampler_col[1] * guided  1.98 us
    add x1, other arithmetic, shards(): offset = time_row + cond_embed[0]  1.87 us
  transfers between devices with their start and end apart: 6, of which 3 were waited for; matrix products, arithmetic and copies ran while one was open for 16% of the time, Pallas kernels for 0%

commit v1 on v0

v1 whole, which is shorter than its diff:
```python
import functools

import jax
import jax.numpy as jnp
from jax import lax
from jax.experimental import pallas as pl
from jax.experimental.pallas import tpu as pltpu
from jax.sharding import PartitionSpec as P

LANES = 128
TILE = 256


def up(value, unit):
    return -(-value // unit) * unit


def turned(field, by, stride):
    return pltpu.roll(field, by % stride, 0)


def spread_taps(ref, base, field, stride, chans):
    rows = field.shape[0] // stride
    for tap in range(3):
        parts = [
            turned(field[k * stride : (k + 1) * stride], 1 - tap, stride) if tap != 1 else field[k * stride : (k + 1) * stride]
            for k in range(rows)
        ]
        for k in range(rows):
            ref[pl.ds(pl.multiple_of(base + k * stride, 16), stride), tap * chans : (tap + 1) * chans] = parts[k].astype(jnp.bfloat16)


def section_kernel(
    geom, coef_ref, lat_ref, win_ref, wide_ref, thin_ref, wout_ref, vec_ref, out_ref,
    state, taps, first, lift, thin, low, mixed,
):
    steps, height, cols, stride, margin, feat, chans = geom
    wide = feat // TILE * TILE
    rest = feat - wide
    row_home = lax.axis_index("band") * height
    image_rows = lax.axis_size("band") * height
    image_cols = lax.axis_size("sub") * lax.axis_size("cfg") * cols
    col_home = (lax.axis_index("sub") * lax.axis_size("cfg") + lax.axis_index("cfg")) * cols - margin

    def inside(row, lanes):
        place = lax.broadcasted_iota(jnp.int32, (stride, lanes), 0) + col_home
        image_row = row_home + row
        limit = jnp.where((image_row >= 0) & (image_row < image_rows), image_cols, 0)
        return (place >= 0) & (place < limit)

    def at(row, count=1):
        return pl.ds(pl.multiple_of(row * stride, 16), count * stride)

    copies = LANES // chans
    tall = jnp.concatenate([lat_ref[...]] * copies, axis=0)
    state[...] = jnp.transpose(tall)
    group = lax.broadcasted_iota(jnp.int32, (stride, LANES), 1) // chans

    for step in range(steps):
        edge = margin - 3 * step
        rows = height + 2 * edge
        firsts = rows - 2
        seconds = rows - 4
        last = step == steps - 1
        scale1 = vec_ref[0:1, :]
        scale2 = vec_ref[1:2, :]
        base = 2 + 4 * step
        shift1 = [vec_ref[base + q : base + q + 1, :] for q in range(2)]
        shift2 = [vec_ref[base + 2 + q : base + 3 + q, :] for q in range(2)]

        def lay(row, carry):
            field = state[at(row), :]
            before = turned(field, 1, stride)
            after = turned(field, -1, stride)
            mixed_row = jnp.where(group % 3 == 0, before, jnp.where(group % 3 == 1, field, after))
            mixed[at(row), 0:LANES] = mixed_row
            mixed[at(row), LANES : 2 * LANES] = after
            return carry

        lax.fori_loop(0, rows, lay, 0)

        def gather(row, carry):
            one = mixed[at(row), 0:LANES]
            two = mixed[at(row + 1), 0:LANES]
            three = mixed[at(row + 2), 0:LANES]
            body = jnp.where(group < 3, one, jnp.where(group < 6, two, three))
            taps[at(row), 0:LANES] = body.astype(jnp.bfloat16)
            taps[at(row), LANES : LANES + chans] = mixed[at(row + 2), LANES : LANES + chans].astype(jnp.bfloat16)
            return carry

        lax.fori_loop(0, firsts, gather, 0)

        def lead(pair, carry):
            row = pair * 2
            field = jnp.dot(taps[at(row, 2), :], win_ref[...], preferred_element_type=jnp.float32)
            first[at(row, 2), :] = field
            for k in range(2):
                keep = inside(row + k + 1 - edge, feat)
                for q in range(2):
                    half = field[k * stride : (k + 1) * stride] * scale1 + shift1[q]
                    value = jnp.where(keep, half + half * jnp.tanh(half), 0.0)
                    spread_taps(lift.at[q], (row + k) * stride, value, stride, feat)
            return carry

        lax.fori_loop(0, firsts // 2, lead, 0)

        chunk = 6 if firsts % 6 == 0 else 2

        def narrow(k, carry):
            for q in range(2):
                thin[q, at(k * chunk, chunk), :] = jnp.dot(
                    lift[q, at(k * chunk, chunk), :], thin_ref[...], preferred_element_type=jnp.float32
                )
            return carry

        lax.fori_loop(0, firsts // chunk, narrow, 0)

        count = 4 if seconds % 4 == 0 else (5 if seconds % 5 == 0 else 2)
        gain = coef_ref[step, 2]

        def middle(k, carry):
            row = k * count
            lowered = None
            for q in range(2):
                total = first[at(row + 1, count), 0:wide]
                for tap in range(3):
                    total = total + jnp.dot(
                        lift[q, at(row + tap, count), :], wide_ref[tap], preferred_element_type=jnp.float32
                    )
                tail = first[at(row + 1, count), wide:feat]
                for tap in range(3):
                    tail = tail + thin[q, at(row + tap, count), tap * rest : (tap + 1) * rest]
                both = []
                for field, part in ((total, slice(0, wide)), (tail, slice(wide, feat))):
                    half = field * scale2[:, part] + shift2[q][:, part]
                    both.append(half + half * jnp.tanh(half))
                if q == 0:
                    lowered = both
                else:
                    lowered = [a + gain * (b - a) for a, b in zip(lowered, both)]
            for part_values, start in zip(lowered, (0, wide)):
                width = part_values.shape[1]
                for m in range(count):
                    keep = inside(row + m + 2 - edge, width)
                    value = jnp.where(keep, part_values[m * stride : (m + 1) * stride], 0.0)
                    for tap in range(3):
                        moved = value if tap == 1 else turned(value, 1 - tap, stride)
                        low[at(row + m), tap * feat + start : tap * feat + start + width] = moved.astype(jnp.bfloat16)
            return carry

        lax.fori_loop(0, seconds // count, middle, 0)

        def close(k, carry):
            mixed2 = jnp.dot(low[at(k * 2, 2), :], wout_ref[...], preferred_element_type=jnp.float32)
            noise[at(k * 2, 2), :] = mixed2
            return carry

        noise = mixed
        lax.fori_loop(0, seconds // 2, close, 0)

        def finish(row, carry):
            total = noise[at(row), 0:LANES]
            total = total + noise[at(row + 1), LANES : 2 * LANES]
            total = total + noise[at(row + 2), 2 * LANES : 3 * LANES]
            value = coef_ref[step, 0] * state[at(row + 3), :] + coef_ref[step, 1] * total
            if not last:
                value = jnp.where(inside(row + 3 - edge, LANES), value, 0.0)
            state[at(row), :] = value
            return carry

        lax.fori_loop(0, rows - 6, finish, 0)

    out_ref[...] = jnp.transpose(state[0 : up(height * stride, LANES), :])[0:chans, :]


def shards(
    latents, in_weight, mid_weight, out_weight, norm_mean, norm_rstd,
    cond_embed, time_embed, time_index, coef_index, sampler_table,
):
    chans, height, full_cols = latents.shape
    feat = in_weight.shape[3]
    steps = time_index.shape[0]
    margin = 3 * steps
    parts = lax.axis_size("cfg")
    subs = lax.axis_size("sub")
    bands = lax.axis_size("band")
    cols = full_cols // parts
    stride = up(cols + 2 * margin, 16)
    rows = height + 2 * margin
    wide = feat // TILE * TILE
    rest = feat - wide
    mine = lax.axis_index("cfg")

    sent = latents.astype(jnp.bfloat16)
    above = lax.ppermute(sent[:, -margin:], "band", [(i, i + 1) for i in range(bands - 1)])
    below = lax.ppermute(sent[:, :margin], "band", [(i + 1, i) for i in range(bands - 1)])
    tall = jnp.concatenate([above.astype(jnp.float32), latents, below.astype(jnp.float32)], axis=1)
    edge = jnp.where(mine == 0, tall[:, :, -margin:], tall[:, :, :margin]).astype(jnp.bfloat16)
    route = [(s * parts, (s + 1) * parts) for s in range(subs - 1)]
    route += [((s + 1) * parts + 1, s * parts + 1) for s in range(subs - 1)]
    beside = lax.ppermute(edge, ("sub", "cfg"), route).astype(jnp.float32)
    window = jnp.where(
        mine == 0,
        jnp.concatenate([beside, tall[:, :, : cols + margin]], axis=2),
        jnp.concatenate([tall[:, :, full_cols - cols - margin :], beside], axis=2),
    )
    window = jnp.pad(window, ((0, 0), (0, 0), (0, stride - cols - 2 * margin)))
    pixels = rows * stride
    held = up(pixels, LANES)
    window = jnp.pad(window.reshape(chans, pixels), ((0, 0), (0, held - pixels)))

    other = lax.ppermute(cond_embed, "cfg", [(0, 1), (1, 0)])
    plain = jnp.where(mine == 0, cond_embed, other)[0]
    steered = jnp.where(mine == 0, other, cond_embed)[0]
    half = 0.5 * norm_rstd
    lines = [half[0], half[1]]
    coefs = []
    for step in range(steps):
        time_row = lax.dynamic_index_in_dim(time_embed, time_index[step], 0, keepdims=False)
        coefs.append(lax.dynamic_index_in_dim(sampler_table, coef_index[step], 1, keepdims=False))
        for layer in range(2):
            for cond in (plain, steered):
                lines.append((time_row + cond - norm_mean[layer]) * half[layer])
    vecs = jnp.stack(lines)
    vecs = jnp.pad(vecs, ((0, up(vecs.shape[0], 8) - vecs.shape[0]), (0, 0)))
    coefs = jnp.stack(coefs)

    win = in_weight.reshape(9 * chans, feat)
    wmid = jnp.transpose(mid_weight, (0, 1, 3, 2)).reshape(3, 3 * feat, feat)
    wwide = wmid[:, :, :wide]
    wthin = jnp.transpose(wmid[:, :, wide:], (1, 0, 2)).reshape(3 * feat, 3 * rest)
    copies = LANES // chans
    wout = jnp.transpose(out_weight, (1, 3, 0, 2)).reshape(3 * feat, 3, 1, chans)
    wout = jnp.broadcast_to(wout, (3 * feat, 3, copies, chans)).reshape(3 * feat, 3 * LANES)

    geom = (steps, height, cols, stride, margin, feat, chans)
    whole = pl.BlockSpec(memory_space=pltpu.VMEM)
    firsts = (rows - 2) * stride
    seconds = (rows - 4) * stride
    out = pl.pallas_call(
        functools.partial(section_kernel, geom),
        out_shape=jax.ShapeDtypeStruct((chans, up(height * stride, LANES)), jnp.float32),
        in_specs=[pl.BlockSpec(memory_space=pltpu.SMEM)] + [whole] * 6,
        out_specs=whole,
        scratch_shapes=[
            pltpu.VMEM((held, LANES), jnp.float32),
            pltpu.VMEM((firsts, 9 * chans), jnp.bfloat16),
            pltpu.VMEM((firsts, feat), jnp.float32),
            pltpu.VMEM((2, firsts, 3 * feat), jnp.bfloat16),
            pltpu.VMEM((2, firsts, 3 * rest), jnp.float32),
            pltpu.VMEM((seconds, 3 * feat), jnp.bfloat16),
            pltpu.VMEM((rows * stride, 3 * LANES), jnp.float32),
        ],
        compiler_params=pltpu.CompilerParams(vmem_limit_bytes=48 * 1024 * 1024),
    )(coefs, window, win, wwide, wthin, wout, vecs)
    out = out[:, : height * stride].reshape(chans, height, stride)[:, :, margin : margin + cols]
    far = lax.ppermute(out, "cfg", [(0, 1), (1, 0)])
    return jnp.where(
        mine == 0, jnp.concatenate([out, far], axis=2), jnp.concatenate([far, out], axis=2)
    )


def solution(mesh):
    return jax.shard_map(
        shards,
        mesh=mesh,
        in_specs=(P("groups", "band", "sub"), P(), P(), P(), P(), P(), P("cfg", "groups"), P(), P(), P(), P()),
        out_specs=P("groups", "band", "sub"),
        check_vma=False,
    )
```

time: 75.8 us -> 65.9 us (0.87)
  the two profiles are of different devices: /device:TPU:0 before, /device:TPU:11 now
where the time goes in v1:
time: 65.9 us; the launch traced here: 65.4 us
  Pallas kernels  26.8 us (41%)
  starting transfers between devices  12 us (18%)
  local copies, waits for them, and re-layouts  11.9 us (18%)
  between operations  8.04 us (12%)
  other arithmetic  4.24 us (6%)
  waiting for transfers between devices  2.41 us (4%)
    pallas_call x1, Pallas kernels, shards(): pl.pallas_call(functools.partial(section_kernel, geom), out_shape=jax.Sha...  26.8 us
    ppermute x1, starting transfers between devices, shards(): far = lax.ppermute(out, 'cfg', [(0, 1), (1, 0)])  3.32 us
    ppermute x1, starting transfers between devices, shards(): lax.ppermute(sent[:, -margin:], 'band', [(i, i + 1) for i in range(bands...  3.19 us
    transpose x1, local copies, waits for them, and re-layouts, shards(): wmid = jnp.transpose(mid_weight, (0, 1, 3, 2)).reshape(3, 3 * feat, feat)  2.99 us
    ppermute x1, starting transfers between devices, shards(): lax.ppermute(sent[:, :margin], 'band', [(i + 1, i) for i in range(bands -...  2.66 us
    ppermute x1, starting transfers between devices, shards(): beside = lax.ppermute(edge, ('sub', 'cfg'), route).astype(jnp.float32)  2.16 us
    slice x1, local copies, waits for them, and re-layouts, shards(): wwide = wmid[:, :, :wide]  1.5 us
    ppermute x1, waiting for transfers between devices, shards(): beside = lax.ppermute(edge, ('sub', 'cfg'), route).astype(jnp.float32)  1.5 us
  transfers between devices with their start and end apart: 5, of which 2 were waited for; matrix products, arithmetic and copies ran while one was open for 21% of the time, Pallas kernels for 0%

profile of v1, /device:TPU:11, one launch (start us, length us, event | category | flops | bytes accessed | tf_op | source)
XLA Modules:
  0.0 65.4 jit_solution(14406754346484576242)
XLA Ops:
  0.0 0.7 %collective-permute-start.3 = (f32[1,320]{1,0:T(1,128)}, f32[1,320]{1,0:T(1,128)S(1)}, u32[]{:S(2)}, u32[]{:S(2)}) collective-permute-start(f32[1,320]{1,0:T(1,128)} %param.17), channel_id=1, source_target_pairs={{0,1},{1,0},{2,3},{3,2},{4,5},{5,4},{6,7},{7,6},{8,9},{9,8},{10,11... | collective-permute-start | bytes 3848 | tf_op jit(solution)/shard_map/ppermute | solution.py:212
  0.7 0.8 %convert_element_type.21 = bf16[16,8,128]{2,1,0:T(8,128)(2,1)S(1)} convert(f32[16,8,128]{2,1,0:T(8,128)} %param.11) | non-fusion elementwise | flops 16384 | bytes 98304 | tf_op jit(solution)/shard_map/convert_element_type | solution.py:194
  1.5 0.6 fusion.2
  2.2 3.2 %collective-permute-start = (bf16[16,6,128]{2,1,0:T(8,128)(2,1)}, bf16[16,6,128]{2,1,0:T(8,128)(2,1)}, u32[]{:S(2)}, u32[]{:S(2)}) collective-permute-start(bf16[16,6,128]{2,1,0:T(8,128)(2,1)} %get-tuple-element.15), channel_id=1, source_target_pairs={{0,4},{4,8},{8,12},{1,5},{5,9},{9,13},{2,6},{6,10},{10,14},{3,7},{... | collective-permute-start | bytes 73736 | tf_op jit(solution)/shard_map/ppermute | solution.py:195
  5.4 2.7 %collective-permute-start.1 = (bf16[16,6,128]{2,1,0:T(8,128)(2,1)}, bf16[16,6,128]{2,1,0:T(8,128)(2,1)S(1)}, u32[]{:S(2)}, u32[]{:S(2)}) collective-permute-start(bf16[16,6,128]{2,1,0:T(8,128)(2,1)} %get-tuple-element.16), channel_id=1, source_target_pairs={{4,0},{8,4},{12,8},{5,1},{9,5},{13,9},{6,2},{10,6},{14,10},{7,3},{... | collective-permute-start | bytes 73736 | tf_op jit(solution)/shard_map/ppermute | solution.py:196
  8.0 1.3 %fusion.3 = (s32[1]{0:T(128)}, s32[1]{0:T(128)}) fusion(s32[2]{0:T(128)} %param.19), kind=kLoop, calls=%fused_computation.24 | loop fusion | bytes 16 | tf_op jit(solution)/shard_map/slice | solution.py:219
  11.9 1.4 %fusion.4 = (s32[1]{0:T(128)}, s32[1]{0:T(128)}) fusion(s32[2]{0:T(128)} %param.20), kind=kLoop, calls=%fused_computation.25 | loop fusion | bytes 16 | tf_op jit(solution)/shard_map/slice | solution.py:220
  15.9 0.7 %broadcast_multiply_fusion = f32[2,320]{1,0:T(2,128)S(1)} fusion(f32[2,320]{1,0:T(2,128)} %param.16), kind=kLoop, calls=%fused_computation.18 | loop fusion | flops 640 | bytes 5120 | tf_op jit(solution)/shard_map/mul | solution.py:215
  16.6 3.0 %copy.16 = bf16[3,3,320,320]{3,2,1,0:T(8,128)(2,1)S(1)} copy(bf16[3,3,320,320]{2,3,1,0:T(8,128)(2,1)} %bitcast.20) | data formatting | bytes 3686400 | tf_op jit(solution)/shard_map/transpose | solution.py:229
  19.6 0.0 copy-start.1
  19.6 0.1 slice_bitcast_fusion
  22.3 1.1 %constant_dynamic-slice_fusion = (f32[1,320]{0,1:T(8,128)S(1)}, f32[1,320]{0,1:T(8,128)S(1)}) fusion(f32[1000,320]{0,1:T(8,128)} %param.18, s32[]{:T(128)S(6)} %select_n.61, s32[]{:T(128)S(6)} %select_n.57), kind=kLoop, calls=%fused_computation.20 | loop fusion | bytes 5128 | tf_op jit(solution)/shard_map/jit(dynamic_index_in_dim)/dynamic_slice | solution.py:219
  23.5 0.9 %dynamic-slice_reduce_fusion.1 = (f32[3]{0:T(128)S(1)}, f32[3]{0:T(128)S(1)}) fusion(f32[3,1000]{1,0:T(4,128)} %param.21, s32[]{:T(128)S(6)} %select_n.51, s32[]{:T(128)S(6)} %select_n.52), kind=kLoop, calls=%fused_computation.9 | loop fusion | bytes 56 | tf_op jit(solution)/shard_map/jit(dynamic_index_in_dim)/dynamic_slice | solution.py:220
  24.4 0.0 copy-done.1
  24.4 0.0 copy-start.2
  24.5 1.5 %slice.89.wide_ref = bf16[3,960,256]{2,1,0:T(8,128)(2,1)S(1)} slice(bf16[3,960,320]{2,1,0:T(8,128)(2,1)} %bitcast.18), slice={[0:3], [0:960], [0:256]} | slice | bytes 2949120 | tf_op jit(solution)/shard_map/slice | solution.py:230
  26.0 0.1 copy.24
  26.0 0.1 copy.23
  26.2 0.0 copy-start.3
  26.2 0.0 copy-start.4
  26.2 0.3 copy.17
  26.5 0.2 copy.21.thin_ref
  26.7 0.0 copy-done.2
  26.7 0.1 copy.18
  26.7 0.1 broadcast_in_dim.7
  26.9 0.1 broadcast_in_dim.8
  27.0 0.4 copy.22.wout_ref
  27.3 0.0 copy-start
  27.4 0.0 collective-permute-done.3
  27.4 0.0 copy-done.3
  27.4 0.0 copy-done.4
  27.4 0.1 stack.24
  27.5 0.0 collective-permute-done
  27.5 0.8 %convert_element_type.22 = f32[16,6,128]{2,1,0:T(8,128)S(1)} convert(bf16[16,6,128]{2,1,0:T(8,128)(2,1)} %collective-permute-done) | non-fusion elementwise | flops 12288 | bytes 73728 | tf_op jit(solution)/shard_map/convert_element_type | solution.py:197
  28.3 0.0 collective-permute-done.1
  28.3 0.9 %pad_maximum_fusion = f32[16,20,128]{2,1,0:T(8,128)S(1)} fusion(f32[16,6,128]{2,1,0:T(8,128)S(1)} %convert_element_type.23, f32[16,8,128]{2,1,0:T(8,128)} %param.11, f32[16,6,128]{2,1,0:T(8,128)S(1)} %convert_element_type.22), kind=kLoop, calls=%fused_computation.3 | loop fusion | flops 81920 | bytes 327680 | tf_op jit(solution)/shard_map/concatenate | solution.py:197
  29.2 0.1 fusion
  29.3 2.2 %collective-permute-start.2 = (bf16[16,20,6]{2,1,0:T(8,128)(2,1)S(1)}, bf16[16,20,6]{2,1,0:T(8,128)(2,1)S(1)}, u32[]{:S(2)}, u32[]{:S(2)}) collective-permute-start(bf16[16,20,6]{2,1,0:T(8,128)(2,1)S(1)} %fusion), channel_id=1, source_target_pairs={{0,2},{3,1},{4,6},{7,5},{8,10},{11,9},{12,14},{15,13},{16,18},{19,... | collective-permute-start | bytes 11528 | tf_op jit(solution)/shard_map/ppermute | solution.py:201
  31.4 0.1 fusion.1
  31.6 1.5 %collective-permute-done.2 = bf16[16,20,6]{2,1,0:T(8,128)(2,1)S(1)} collective-permute-done((bf16[16,20,6]{2,1,0:T(8,128)(2,1)S(1)}, bf16[16,20,6]{2,1,0:T(8,128)(2,1)S(1)}, u32[]{:S(2)}, u32[]{:S(2)}) %collective-permute-start.2) | collective-permute-done | bytes 3872 | tf_op jit(solution)/shard_map/ppermute | solution.py:201
  33.1 0.2 maximum_select_fusion
  33.3 0.1 reshape.22
  33.4 0.0 copy-done
  33.4 26.8 %shard_map.109 = f32[16,640]{1,0:T(8,128)S(1)} custom-call(f32[2,3]{1,0:T(2,128)S(1)} %pad_maximum_fusion.1.coef_ref, f32[16,1664]{1,0:T(8,128)S(1)} %pad.13.lat_ref, bf16[144,320]{1,0:T(8,128)(2,1)S(1)} %bitcast.16, bf16[3,960,256]{2,1,0:T(8,128)(2,1)S(1)} %slice.89.wide_ref, bf16[960,192]{1,0:T(8,128)(2,1)S(1)} %copy.21.thin_ref, ...), custom_call_target="tpu_custom_call" | custom-call | tf_op jit(solution)/shard_map/pallas_call | solution.py:240
  60.2 0.1 reshape.27
  60.3 0.1 slice.93
  60.4 3.3 %collective-permute-start.4 = (f32[16,8,64]{2,1,0:T(8,128)S(1)}, f32[16,8,64]{2,1,0:T(8,128)S(1)}, u32[]{:S(2)}, u32[]{:S(2)}) collective-permute-start(f32[16,8,64]{2,1,0:T(8,128)S(1)} %slice.93), channel_id=1, source_target_pairs={{0,1},{1,0},{2,3},{3,2},{4,5},{5,4},{6,7},{7,6},{8,9},{9,8},{10,11... | collective-permute-start | bytes 98312 | tf_op jit(solution)/shard_map/ppermute | solution.py:257
  63.7 0.9 %collective-permute-done.4 = f32[16,8,64]{2,1,0:T(8,128)S(1)} collective-permute-done((f32[16,8,64]{2,1,0:T(8,128)S(1)}, f32[16,8,64]{2,1,0:T(8,128)S(1)}, u32[]{:S(2)}, u32[]{:S(2)}) %collective-permute-start.4) | collective-permute-done | bytes 32800 | tf_op jit(solution)/shard_map/ppermute | solution.py:257
  64.6 0.7 %maximum_select_fusion.1 = f32[16,8,128]{2,1,0:T(8,128)} fusion(f32[16,8,64]{2,1,0:T(8,128)S(1)} %collective-permute-done.4, f32[16,8,64]{2,1,0:T(8,128)S(1)} %slice.93, pred[]{:T(512)S(6)} %eq.2), kind=kLoop, calls=%fused_computation.5 | loop fusion | flops 49152 | bytes 131073 | tf_op jit(solution)/shard_map/jit(_where)/select_n | solution.py:258
  (8 shorter events, 0.1 us)
Async XLA Ops:
  0.0 27.4 %collective-permute-start.3 = (f32[1,320]{1,0:T(1,128)}, f32[1,320]{1,0:T(1,128)S(1)}, u32[]{:S(2)}, u32[]{:S(2)}) collective-permute-start(f32[1,320]{1,0:T(1,128)} %param.17), channel_id=1, source_target_pairs={{0,1},{1,0},{2,3},{3,2},{4,5},{5,4},{6,7},{7,6},{8,9},{9,8},{10,11... | collective-permute-start | bytes 3848 | tf_op jit(solution)/shard_map/ppermute | solution.py:212
  2.2 25.3 %collective-permute-start = (bf16[16,6,128]{2,1,0:T(8,128)(2,1)}, bf16[16,6,128]{2,1,0:T(8,128)(2,1)}, u32[]{:S(2)}, u32[]{:S(2)}) collective-permute-start(bf16[16,6,128]{2,1,0:T(8,128)(2,1)} %get-tuple-element.15), channel_id=1, source_target_pairs={{0,4},{4,8},{8,12},{1,5},{5,9},{9,13},{2,6},{6,10},{10,14},{3,7},{... | collective-permute-start | bytes 73736 | tf_op jit(solution)/shard_map/ppermute | solution.py:195
  5.4 22.9 %collective-permute-start.1 = (bf16[16,6,128]{2,1,0:T(8,128)(2,1)}, bf16[16,6,128]{2,1,0:T(8,128)(2,1)S(1)}, u32[]{:S(2)}, u32[]{:S(2)}) collective-permute-start(bf16[16,6,128]{2,1,0:T(8,128)(2,1)} %get-tuple-element.16), channel_id=1, source_target_pairs={{4,0},{8,4},{12,8},{5,1},{9,5},{13,9},{6,2},{10,6},{14,10},{7,3},{... | collective-permute-start | bytes 73736 | tf_op jit(solution)/shard_map/ppermute | solution.py:196
  19.6 4.8 %copy-start.1 = (bf16[3,3,320,320]{3,2,1,0:T(8,128)(2,1)}, bf16[3,3,320,320]{3,2,1,0:T(8,128)(2,1)S(1)}, u32[]{:S(2)}) copy-start(bf16[3,3,320,320]{3,2,1,0:T(8,128)(2,1)S(1)} %copy.16) | copy-start | bytes 5529604
  24.4 2.2 %copy-start.2 = (bf16[3,3,16,320]{3,2,1,0:T(8,128)(2,1)S(1)}, bf16[3,3,16,320]{3,2,1,0:T(8,128)(2,1)}, u32[]{:S(2)}) copy-start(bf16[3,3,16,320]{3,2,1,0:T(8,128)(2,1)} %param.14) | copy-start | bytes 276484
  26.2 1.2 %copy-start.3 = (f32[2,320]{1,0:T(2,128)S(1)}, f32[2,320]{1,0:T(2,128)}, u32[]{:S(2)}) copy-start(f32[2,320]{1,0:T(2,128)} %param.15) | copy-start | bytes 7684
  26.2 1.2 %copy-start.4 = (f32[1,320]{1,0:T(1,128)S(1)}, f32[1,320]{1,0:T(1,128)}, u32[]{:S(2)}) copy-start(f32[1,320]{1,0:T(1,128)} %param.17) | copy-start | bytes 3844
  27.3 6.1 %copy-start = (bf16[3,3,16,320]{3,2,1,0:T(8,128)(2,1)S(1)}, bf16[3,3,16,320]{3,2,1,0:T(8,128)(2,1)}, u32[]{:S(2)}) copy-start(bf16[3,3,16,320]{3,2,1,0:T(8,128)(2,1)} %param.12) | copy-start | bytes 276484
  29.3 3.8 %collective-permute-start.2 = (bf16[16,20,6]{2,1,0:T(8,128)(2,1)S(1)}, bf16[16,20,6]{2,1,0:T(8,128)(2,1)S(1)}, u32[]{:S(2)}, u32[]{:S(2)}) collective-permute-start(bf16[16,20,6]{2,1,0:T(8,128)(2,1)S(1)} %fusion), channel_id=1, source_target_pairs={{0,2},{3,1},{4,6},{7,5},{8,10},{11,9},{12,14},{15,13},{16,18},{19,... | collective-permute-start | bytes 11528 | tf_op jit(solution)/shard_map/ppermute | solution.py:201
  60.4 4.2 %collective-permute-start.4 = (f32[16,8,64]{2,1,0:T(8,128)S(1)}, f32[16,8,64]{2,1,0:T(8,128)S(1)}, u32[]{:S(2)}, u32[]{:S(2)}) collective-permute-start(f32[16,8,64]{2,1,0:T(8,128)S(1)} %slice.93), channel_id=1, source_target_pairs={{0,1},{1,0},{2,3},{3,2},{4,5},{5,4},{6,7},{7,6},{8,9},{9,8},{10,11... | collective-permute-start | bytes 98312 | tf_op jit(solution)/shard_map/ppermute | solution.py:257

commit v2 on v1

v2 whole, which is shorter than its diff:
```python
import functools

import jax
import jax.numpy as jnp
from jax import lax
from jax.experimental import pallas as pl
from jax.experimental.pallas import tpu as pltpu
from jax.sharding import PartitionSpec as P

LANES = 128
TILE = 256
MESH = pl.DeviceIdType.MESH


def up(value, unit):
    return -(-value // unit) * unit


def turned(field, tap):
    return field if tap == 1 else pltpu.roll(field, (1 - tap) % field.shape[0], 0)


def section_kernel(
    geom, time_at, coef_at, table, lat_ref, win_ref, mid_hbm, wout_ref, mean_ref, rstd_ref, cond_ref, time_hbm, out_ref,
    state, taps, first, lift0, lift1, thin0, thin1, low, mixed,
    mid_ref, time_ref, wide_ref, narrow_ref, last_ref, vec_ref,
    row_send, row_recv, col_send, col_recv, cond_recv, half_send, half_recv,
    local_sem, send_sem, recv_sem,
):
    steps, height, full_cols, cols, stride, margin, feat, chans = geom
    wide = feat // TILE * TILE
    rest = feat - wide
    depth = 3 * wide + up(3 * rest, TILE)
    side = (stride - cols) // 2
    lifts = (lift0, lift1)
    thins = (thin0, thin1)
    band, sub, mine = (lax.axis_index(name) for name in ("band", "sub", "cfg"))
    bands, subs, parts = (lax.axis_size(name) for name in ("band", "sub", "cfg"))
    row_home = band * height
    image_rows = bands * height
    image_cols = subs * parts * cols
    col_home = (sub * parts + mine) * cols - side
    first_core = mine == 0

    def inside(row, lanes):
        place = lax.broadcasted_iota(jnp.int32, (stride, lanes), 0) + col_home
        image_row = row_home + row
        limit = jnp.where((image_row >= 0) & (image_row < image_rows), image_cols, 0)
        return (place >= 0) & (place < limit)

    def at(row, count=1):
        return pl.ds(pl.multiple_of(row * stride, 16), count * stride)

    ahead = jnp.where(first_core, sub + 1, sub - 1)
    behind = jnp.where(first_core, sub - 1, sub + 1)
    goes = (ahead >= 0) & (ahead < subs)
    comes = (behind >= 0) & (behind < subs)
    has_up = band > 0
    has_down = band < bands - 1
    partner = {"cfg": 1 - mine}

    mid_copy = pltpu.make_async_copy(mid_hbm, mid_ref, local_sem.at[0])
    time_copy = pltpu.make_async_copy(time_hbm, time_ref, local_sem.at[1])
    mid_copy.start()
    time_copy.start()

    barrier = pltpu.get_barrier_semaphore()

    def greet(when, device):
        @pl.when(when)
        def _():
            pl.semaphore_signal(barrier, inc=1, device_id=device, device_id_type=MESH)

    greet(has_up, {"band": band - 1})
    greet(has_down, {"band": band + 1})
    greet(comes, {"sub": behind})
    greet(comes & has_up, {"band": band - 1, "sub": behind})
    greet(comes & has_down, {"band": band + 1, "sub": behind})
    pl.semaphore_signal(barrier, inc=1, device_id=partner, device_id_type=MESH)

    copies = LANES // chans
    for y in range(height):
        row_send[y * chans : (y + 1) * chans, :] = lat_ref[:, y, :].astype(jnp.bfloat16)

    def stand(block):
        return jnp.transpose(jnp.concatenate([block] * copies, axis=0))

    bodies = [stand(lat_ref[:, y, :]) for y in range(height)]
    for y in range(0, height, 2):
        pair = [
            jnp.where(first_core, bodies[y + k][full_cols - side :], bodies[y + k][:side]) for k in range(2)
        ]
        col_send[y * side : (y + 2) * side, :] = jnp.concatenate(pair, axis=0).astype(jnp.bfloat16)

    def count(flag):
        return flag.astype(jnp.int32)

    pl.semaphore_wait(
        barrier,
        1 + count(has_up) + count(has_down) + count(goes) + count(goes & has_up) + count(goes & has_down),
    )

    rows = height + 2 * margin
    row_part = margin * chans
    col_part = margin * side

    def remote(k, source, target, device):
        return pltpu.make_async_remote_copy(
            src_ref=source, dst_ref=target, send_sem=send_sem.at[k], recv_sem=recv_sem.at[k],
            device_id=device, device_id_type=MESH,
        )

    row_all = height * chans
    col_all = height * side
    sends = [
        (has_down, has_up, remote(0, row_send.at[row_all - row_part : row_all], row_recv.at[0:row_part], {"band": band + 1})),
        (has_up, has_down, remote(1, row_send.at[0:row_part], row_recv.at[row_part : 2 * row_part], {"band": band - 1})),
        (goes, comes, remote(2, col_send, col_recv.at[col_part : col_part + col_all], {"sub": ahead})),
        (goes & has_down, comes & has_up, remote(3, col_send.at[col_all - col_part : col_all], col_recv.at[0:col_part], {"band": band + 1, "sub": ahead})),
        (goes & has_up, comes & has_down, remote(4, col_send.at[0:col_part], col_recv.at[col_part + col_all : 2 * col_part + col_all], {"band": band - 1, "sub": ahead})),
    ]
    for go, come, copy in sends:
        pl.when(go)(copy.start)
    cond_copy = remote(5, cond_ref, cond_recv, partner)
    cond_copy.start()

    mid_copy.wait()
    for i in range(3):
        for j in range(3):
            turned_mid = jnp.transpose(mid_ref[i, j].astype(jnp.float32)).astype(jnp.bfloat16)
            base = i * depth
            wide_ref[base + j * wide : base + (j + 1) * wide, :] = turned_mid[:wide, :wide]
            narrow_ref[j * wide : (j + 1) * wide, i * rest : (i + 1) * rest] = turned_mid[:wide, wide:]
            spot = 3 * wide + j * rest
            wide_ref[base + spot : base + spot + rest, :] = turned_mid[wide:, :wide]
            narrow_ref[spot : spot + rest, i * rest : (i + 1) * rest] = turned_mid[wide:, wide:]
            small = wout_ref[i, j].astype(jnp.float32)
            tall = jnp.transpose(jnp.concatenate([small] * copies, axis=0)).astype(jnp.bfloat16)
            last_ref[j * wide : (j + 1) * wide, i * LANES : (i + 1) * LANES] = tall[:wide]
            last_ref[spot : spot + rest, i * LANES : (i + 1) * LANES] = tall[wide:]
        spare = 3 * wide + 3 * rest
        wide_ref[i * depth + spare : (i + 1) * depth, :] = jnp.zeros((depth - spare, wide), jnp.bfloat16)
    narrow_ref[spare:, :] = jnp.zeros((depth - spare, 3 * rest), jnp.bfloat16)
    last_ref[spare:, :] = jnp.zeros((depth - spare, 3 * LANES), jnp.bfloat16)

    cond_copy.wait()
    time_copy.wait()
    plain = jnp.where(first_core, cond_ref[...], cond_recv[...])
    steered = jnp.where(first_core, cond_recv[...], cond_ref[...])
    half_rstd = 0.5 * rstd_ref[...]
    vec_ref[0:2, :] = half_rstd
    for step in range(steps):
        time_row = time_ref[pl.ds(time_at[step], 1), :]
        for layer in range(2):
            for q, cond in enumerate((plain, steered)):
                line = 2 + 4 * step + 2 * layer + q
                vec_ref[line : line + 1, :] = (time_row + cond - mean_ref[layer : layer + 1, :]) * half_rstd[layer : layer + 1, :]

    def wait_for(copy):
        def both():
            copy.wait_recv()

        return both

    for go, come, copy in sends:
        pl.when(go)(copy.wait_send)
        pl.when(come)(wait_for(copy))

    for row in range(rows):
        if margin <= row < margin + height:
            body = bodies[row - margin]
        else:
            spot = row if row < margin else row - height
            body = stand(row_recv[spot * chans : (spot + 1) * chans, :].astype(jnp.float32))
        pair = col_recv[row // 2 * 2 * side : (row // 2 * 2 + 2) * side, :].astype(jnp.float32)
        border = pair[row % 2 * side : (row % 2 + 1) * side]
        field = jnp.where(
            first_core,
            jnp.concatenate([border, body[: cols + side]], axis=0),
            jnp.concatenate([body[full_cols - cols - side :], border], axis=0),
        )
        state[row * stride : (row + 1) * stride, :] = jnp.where(inside(row - margin, LANES), field, 0.0)

    group = lax.broadcasted_iota(jnp.int32, (stride, LANES), 1) // chans

    def silu_of(half):
        return half + half * jnp.tanh(half)

    def spread(ref, row, big, small):
        for tap in range(3):
            ref[at(row), tap * wide : (tap + 1) * wide] = turned(big, tap).astype(jnp.bfloat16)
        ends = [turned(small, tap) for tap in range(3)]
        ends.append(jnp.zeros((stride, depth - 3 * wide - 3 * rest), jnp.float32))
        ref[at(row), 3 * wide : depth] = jnp.concatenate(ends, axis=1).astype(jnp.bfloat16)

    for step in range(steps):
        edge = margin - 3 * step
        now_rows = height + 2 * edge
        firsts = now_rows - 2
        seconds = now_rows - 4
        is_last = step == steps - 1
        base = 2 + 4 * step

        def lay(row, carry):
            field = state[at(row), :]
            before = turned(field, 0)
            after = turned(field, 2)
            mixed[at(row), 0:LANES] = jnp.where(group % 3 == 0, before, jnp.where(group % 3 == 1, field, after))
            mixed[at(row), LANES : 2 * LANES] = after
            return carry

        lax.fori_loop(0, now_rows, lay, 0)

        chunk = 6 if firsts % 6 == 0 else 2

        def lead(k, carry):
            row = k * chunk
            for m in range(chunk):
                one = mixed[at(row + m), 0:LANES]
                two = mixed[at(row + m + 1), 0:LANES]
                three = mixed[at(row + m + 2), 0:LANES]
                body = jnp.where(group < 3, one, jnp.where(group < 6, two, three))
                taps[at(m), 0:LANES] = body.astype(jnp.bfloat16)
                taps[at(m), LANES : LANES + chans] = mixed[at(row + m + 2), LANES : LANES + chans].astype(jnp.bfloat16)
            field = jnp.dot(taps[...][: chunk * stride], win_ref[...], preferred_element_type=jnp.float32)
            first[at(row, chunk), :] = field
            for q in range(2):
                shift = vec_ref[base + q : base + q + 1, :]
                for m in range(chunk):
                    here = field[m * stride : (m + 1) * stride]
                    keep = inside(row + m + 1 - edge, wide)
                    parts = []
                    for part in (slice(0, wide), slice(wide, feat)):
                        value = silu_of(here[:, part] * vec_ref[0:1, part] + shift[:, part])
                        parts.append(jnp.where(keep[:, : value.shape[1]], value, 0.0))
                    spread(lifts[q], row + m, *parts)
                thins[q][at(row, chunk), :] = jnp.dot(
                    lifts[q][at(row, chunk), :], narrow_ref[...], preferred_element_type=jnp.float32
                )
            return carry

        lax.fori_loop(0, firsts // chunk, lead, 0)

        count2 = 4 if seconds % 4 == 0 else (5 if seconds % 5 == 0 else 2)
        gain = table[2, coef_at[step]]

        def middle(k, carry):
            row = k * count2
            found = []
            for q in range(2):
                window = jnp.concatenate([lifts[q][at(row + tap, count2), :] for tap in range(3)], axis=1)
                total = first[at(row + 1, count2), 0:wide] + jnp.dot(
                    window, wide_ref[...], preferred_element_type=jnp.float32
                )
                tail = first[at(row + 1, count2), wide:feat]
                for tap in range(3):
                    tail = tail + thins[q][at(row + tap, count2), tap * rest : (tap + 1) * rest]
                shift = vec_ref[base + 2 + q : base + 3 + q, :]
                found.append(
                    [
                        silu_of(field * vec_ref[1:2, part] + shift[:, part])
                        for field, part in ((total, slice(0, wide)), (tail, slice(wide, feat)))
                    ]
                )
            lowered = [a + gain * (b - a) for a, b in zip(*found)]
            for m in range(count2):
                keep = inside(row + m + 2 - edge, wide)
                spread(
                    low,
                    row + m,
                    *[
                        jnp.where(keep[:, : part.shape[1]], part[m * stride : (m + 1) * stride], 0.0)
                        for part in lowered
                    ],
                )
            mixed[at(row, count2), :] = jnp.dot(low[at(row, count2), :], last_ref[...], preferred_element_type=jnp.float32)
            return carry

        lax.fori_loop(0, seconds // count2, middle, 0)

        keeps = table[0, coef_at[step]]
        adds = table[1, coef_at[step]]

        def finish(row, carry):
            total = mixed[at(row), 0:LANES] + mixed[at(row + 1), LANES : 2 * LANES]
            total = total + mixed[at(row + 2), 2 * LANES : 3 * LANES]
            value = keeps * state[at(row + 3), :] + adds * total
            if not is_last:
                value = jnp.where(inside(row + 3 - edge, LANES), value, 0.0)
            state[at(row), :] = value
            return carry

        lax.fori_loop(0, now_rows - 6, finish, 0)

    group = lax.broadcasted_iota(jnp.int32, (cols, LANES), 1) // chans
    packed = state[side : side + cols, :]
    for y in range(1, height):
        packed = jnp.where(group == y, state[y * stride + side : y * stride + side + cols, :], packed)
    half_send[...] = packed
    swap = remote(6, half_send, half_recv, partner)
    swap.start()
    swap.wait()
    other = half_recv[...]
    joined = jnp.concatenate(
        [jnp.where(first_core, packed, other), jnp.where(first_core, other, packed)], axis=0
    )
    flat = jnp.transpose(joined)
    for y in range(height):
        out_ref[y] = flat[y * chans : (y + 1) * chans]


def shards(
    latents, in_weight, mid_weight, out_weight, norm_mean, norm_rstd,
    cond_embed, time_embed, time_index, coef_index, sampler_table,
):
    chans, height, full_cols = latents.shape
    feat = in_weight.shape[3]
    steps = time_index.shape[0]
    margin = 3 * steps
    cols = full_cols // lax.axis_size("cfg")
    stride = up(cols + 2 * margin, 16)
    side = (stride - cols) // 2
    rows = height + 2 * margin
    wide = feat // TILE * TILE
    rest = feat - wide
    depth = 3 * wide + up(3 * rest, TILE)
    win = in_weight.reshape(9 * chans, feat)
    geom = (steps, height, full_cols, cols, stride, margin, feat, chans)
    whole = pl.BlockSpec(memory_space=pltpu.VMEM)
    scalars = pl.BlockSpec(memory_space=pltpu.SMEM)
    far = pl.BlockSpec(memory_space=pl.ANY)
    firsts = (rows - 2) * stride
    seconds = (rows - 4) * stride
    out = pl.pallas_call(
        functools.partial(section_kernel, geom),
        out_shape=jax.ShapeDtypeStruct((height, chans, full_cols), jnp.float32),
        in_specs=[scalars] * 3 + [whole, whole, far, whole, whole, whole, whole, far],
        out_specs=whole,
        scratch_shapes=[
            pltpu.VMEM((rows * stride, LANES), jnp.float32),
            pltpu.VMEM((6 * stride, 9 * chans), jnp.bfloat16),
            pltpu.VMEM((firsts, feat), jnp.float32),
            pltpu.VMEM((firsts, depth), jnp.bfloat16),
            pltpu.VMEM((firsts, depth), jnp.bfloat16),
            pltpu.VMEM((firsts, 3 * rest), jnp.float32),
            pltpu.VMEM((firsts, 3 * rest), jnp.float32),
            pltpu.VMEM((seconds, depth), jnp.bfloat16),
            pltpu.VMEM((rows * stride, 3 * LANES), jnp.float32),
            pltpu.VMEM(mid_weight.shape, mid_weight.dtype),
            pltpu.VMEM(time_embed.shape, time_embed.dtype),
            pltpu.VMEM((3 * depth, wide), jnp.bfloat16),
            pltpu.VMEM((depth, 3 * rest), jnp.bfloat16),
            pltpu.VMEM((depth, 3 * LANES), jnp.bfloat16),
            pltpu.VMEM((up(2 + 4 * steps, 8), feat), jnp.float32),
            pltpu.VMEM((height * chans, full_cols), jnp.bfloat16),
            pltpu.VMEM((2 * margin * chans, full_cols), jnp.bfloat16),
            pltpu.VMEM((height * side, LANES), jnp.bfloat16),
            pltpu.VMEM((rows * side, LANES), jnp.bfloat16),
            pltpu.VMEM(cond_embed.shape, jnp.float32),
            pltpu.VMEM((cols, LANES), jnp.float32),
            pltpu.VMEM((cols, LANES), jnp.float32),
            pltpu.SemaphoreType.DMA((2,)),
            pltpu.SemaphoreType.DMA((7,)),
            pltpu.SemaphoreType.DMA((7,)),
        ],
        compiler_params=pltpu.CompilerParams(
            vmem_limit_bytes=48 * 1024 * 1024, collective_id=0, has_side_effects=True
        ),
    )(
        time_index, coef_index, sampler_table, latents, win, mid_weight, out_weight,
        norm_mean, norm_rstd, cond_embed, time_embed,
    )
    return jnp.transpose(out, (1, 0, 2))


def solution(mesh):
    return jax.shard_map(
        shards,
        mesh=mesh,
        in_specs=(P("groups", "band", "sub"), P(), P(), P(), P(), P(), P("cfg", "groups"), P(), P(), P(), P()),
        out_specs=P("groups", "band", "sub"),
        check_vma=False,
    )
```

time: 65.9 us -> 36.1 us (0.55)
  the two profiles are of different devices: /device:TPU:11 before, /device:TPU:0 now
where the time goes in v2:
time: 36.1 us; the launch traced here: 36 us
  Pallas kernels  31.6 us (88%)
  local copies, waits for them, and re-layouts  4.19 us (12%)
    pallas_call x1, Pallas kernels, shards(): pl.pallas_call(functools.partial(section_kernel, geom), out_shape=jax.Sha...  31.6 us
    unnamed x21, local copies, waits for them, and re-layouts  3.54 us

profile of v2, /device:TPU:0, one launch (start us, length us, event | category | flops | bytes accessed | tf_op | source)
XLA Modules:
  0.0 36.0 jit_solution(8592298458040430331)
XLA Ops:
  0.0 0.0 copy-start.4
  0.0 0.0 copy-start.9
  0.0 0.0 copy-start.8
  0.0 0.0 copy-start.7
  0.0 0.0 copy-start.6
  0.0 0.0 copy-start.5
  0.0 0.0 copy-start.2
  0.0 0.0 copy-start.1
  0.0 0.0 copy-start.3
  0.1 1.9 %copy.12.time_hbm = f32[1000,320]{1,0:T(8,128)S(1)} copy(f32[1000,320]{0,1:T(8,128)} %param.18) | data formatting | bytes 2560000 | tf_op args[7]
  1.9 0.0 copy-done.4
  2.0 0.0 copy-done.9
  2.0 0.0 copy-done.8
  2.0 0.0 copy-done.7
  2.0 0.0 copy-done.6
  2.0 0.0 copy-done.5
  2.0 0.0 copy-done.2
  2.0 0.0 copy-done.1
  2.0 0.0 copy-done.3
  2.0 0.0 copy-start
  2.1 1.6 %copy-done = bf16[3,3,320,320]{3,2,1,0:T(8,128)(2,1)S(1)} copy-done((bf16[3,3,320,320]{3,2,1,0:T(8,128)(2,1)S(1)}, bf16[3,3,320,320]{3,2,1,0:T(8,128)(2,1)}, u32[]{:S(2)}) %copy-start) | copy-done | bytes 1843224
  3.7 31.6 %shard_map.109 = f32[8,16,128]{2,1,0:T(8,128)S(1)} custom-call(s32[2]{0:T(128)S(1)} %copy-done.8, s32[2]{0:T(128)S(1)} %copy-done.9, f32[3,1000]{1,0:T(4,128)S(1)} %copy-done.4, f32[16,8,128]{2,1,0:T(8,128)S(1)} %copy-done.3, bf16[144,320]{1,0:T(8,128)(2,1)S(1)} %bitcast.3, bf16[3,3,320,320]{3,2,1,0:T(8,128)(2,1)S(1)} %copy-done, ...), custom_call_target="tpu_custom_call" | custom-call | tf_op jit(solution)/shard_map/pallas_call | solution.py:334
  35.3 0.7 %copy.13 = f32[16,8,128]{2,1,0:T(8,128)} copy(f32[16,8,128]{2,0,1:T(8,128)S(1)} %bitcast.2) | data formatting | bytes 131072 | tf_op jit(solution)/shard_map/transpose | solution.py:373
Async XLA Ops:
  0.0 1.9 %copy-start.4 = (f32[3,1000]{1,0:T(4,128)S(1)}, f32[3,1000]{1,0:T(4,128)}, u32[]{:S(2)}) copy-start(f32[3,1000]{1,0:T(4,128)} %table.1) | copy-start | bytes 36004
  0.0 2.0 %copy-start.9 = (s32[2]{0:T(128)S(1)}, s32[2]{0:T(128)}, u32[]{:S(2)}) copy-start(s32[2]{0:T(128)} %coef_at.1) | copy-start | bytes 28
  0.0 2.0 %copy-start.8 = (s32[2]{0:T(128)S(1)}, s32[2]{0:T(128)}, u32[]{:S(2)}) copy-start(s32[2]{0:T(128)} %time_at.1) | copy-start | bytes 28
  0.0 2.0 %copy-start.7 = (f32[1,320]{1,0:T(1,128)S(1)}, f32[1,320]{1,0:T(1,128)}, u32[]{:S(2)}) copy-start(f32[1,320]{1,0:T(1,128)} %cond_ref.1) | copy-start | bytes 3844
  0.0 2.0 %copy-start.6 = (f32[2,320]{1,0:T(2,128)S(1)}, f32[2,320]{1,0:T(2,128)}, u32[]{:S(2)}) copy-start(f32[2,320]{1,0:T(2,128)} %rstd_ref.1) | copy-start | bytes 7684
  0.0 2.0 %copy-start.5 = (f32[2,320]{1,0:T(2,128)S(1)}, f32[2,320]{1,0:T(2,128)}, u32[]{:S(2)}) copy-start(f32[2,320]{1,0:T(2,128)} %mean_ref.1) | copy-start | bytes 7684
  0.0 2.0 %copy-start.2 = (bf16[3,3,16,320]{3,2,1,0:T(8,128)(2,1)S(1)}, bf16[3,3,16,320]{3,2,1,0:T(8,128)(2,1)}, u32[]{:S(2)}) copy-start(bf16[3,3,16,320]{3,2,1,0:T(8,128)(2,1)} %wout_ref.1) | copy-start | bytes 276484
  0.0 2.0 %copy-start.1 = (bf16[3,3,16,320]{3,2,1,0:T(8,128)(2,1)S(1)}, bf16[3,3,16,320]{3,2,1,0:T(8,128)(2,1)}, u32[]{:S(2)}) copy-start(bf16[3,3,16,320]{3,2,1,0:T(8,128)(2,1)} %param.12) | copy-start | bytes 276484
  0.0 2.0 %copy-start.3 = (f32[16,8,128]{2,1,0:T(8,128)S(1)}, f32[16,8,128]{2,1,0:T(8,128)}, u32[]{:S(2)}) copy-start(f32[16,8,128]{2,1,0:T(8,128)} %lat_ref.1) | copy-start | bytes 196612
  2.0 1.6 %copy-start = (bf16[3,3,320,320]{3,2,1,0:T(8,128)(2,1)S(1)}, bf16[3,3,320,320]{3,2,1,0:T(8,128)(2,1)}, u32[]{:S(2)}) copy-start(bf16[3,3,320,320]{3,2,1,0:T(8,128)(2,1)} %mid_hbm.1) | copy-start | bytes 5529604

commit v3 on v2

--- a/solution.py
+++ b/solution.py
@@ -24,7 +24,7 @@
     geom, time_at, coef_at, table, lat_ref, win_ref, mid_hbm, wout_ref, mean_ref, rstd_ref, cond_ref, time_hbm, out_ref,
     state, taps, first, lift0, lift1, thin0, thin1, low, mixed,
     mid_ref, time_ref, wide_ref, narrow_ref, last_ref, vec_ref,
-    row_send, row_recv, col_send, col_recv, cond_recv, half_send, half_recv,
+    row_send, row_recv, col_send, col_recv, cond_recv, half_send, half_recv, outside_ref,
     local_sem, send_sem, recv_sem,
 ):
     steps, height, full_cols, cols, stride, margin, feat, chans = geom
@@ -42,11 +42,13 @@
     col_home = (sub * parts + mine) * cols - side
     first_core = mine == 0
 
+    place = lax.broadcasted_iota(jnp.int32, (stride, wide), 0) + col_home
+    outside_ref[...] = jnp.where((place >= 0) & (place < image_cols), 0, 1)
+
     def inside(row, lanes):
-        place = lax.broadcasted_iota(jnp.int32, (stride, lanes), 0) + col_home
         image_row = row_home + row
-        limit = jnp.where((image_row >= 0) & (image_row < image_rows), image_cols, 0)
-        return (place >= 0) & (place < limit)
+        limit = jnp.where((image_row >= 0) & (image_row < image_rows), 1, 0)
+        return outside_ref[:, :lanes] < limit
 
     def at(row, count=1):
         return pl.ds(pl.multiple_of(row * stride, 16), count * stride)
@@ -127,7 +129,7 @@
     mid_copy.wait()
     for i in range(3):
         for j in range(3):
-            turned_mid = jnp.transpose(mid_ref[i, j].astype(jnp.float32)).astype(jnp.bfloat16)
+            turned_mid = jnp.transpose(mid_ref[i, j])
             base = i * depth
             wide_ref[base + j * wide : base + (j + 1) * wide, :] = turned_mid[:wide, :wide]
             narrow_ref[j * wide : (j + 1) * wide, i * rest : (i + 1) * rest] = turned_mid[:wide, wide:]
@@ -136,12 +138,14 @@
             narrow_ref[spot : spot + rest, i * rest : (i + 1) * rest] = turned_mid[wide:, wide:]
             small = wout_ref[i, j].astype(jnp.float32)
             tall = jnp.transpose(jnp.concatenate([small] * copies, axis=0)).astype(jnp.bfloat16)
-            last_ref[j * wide : (j + 1) * wide, i * LANES : (i + 1) * LANES] = tall[:wide]
-            last_ref[spot : spot + rest, i * LANES : (i + 1) * LANES] = tall[wide:]
+            span = slice(i * LANES // 2, (i + 1) * LANES // 2) if i < 2 else slice(LANES, 2 * LANES)
+            tall = tall[:, : span.stop - span.start]
+            last_ref[j * wide : (j + 1) * wide, span] = tall[:wide]
+            last_ref[spot : spot + rest, span] = tall[wide:]
         spare = 3 * wide + 3 * rest
         wide_ref[i * depth + spare : (i + 1) * depth, :] = jnp.zeros((depth - spare, wide), jnp.bfloat16)
     narrow_ref[spare:, :] = jnp.zeros((depth - spare, 3 * rest), jnp.bfloat16)
-    last_ref[spare:, :] = jnp.zeros((depth - spare, 3 * LANES), jnp.bfloat16)
+    last_ref[spare:, :] = jnp.zeros((depth - spare, 2 * LANES), jnp.bfloat16)
 
     cond_copy.wait()
     time_copy.wait()
@@ -149,8 +153,10 @@
     steered = jnp.where(first_core, cond_recv[...], cond_ref[...])
     half_rstd = 0.5 * rstd_ref[...]
     vec_ref[0:2, :] = half_rstd
+    moments = lax.broadcasted_iota(jnp.int32, time_ref.shape, 1)
     for step in range(steps):
-        time_row = time_ref[pl.ds(time_at[step], 1), :]
+        column = jnp.sum(jnp.where(moments == time_at[step], time_ref[...], 0.0), axis=1, keepdims=True)
+        time_row = jnp.transpose(jnp.broadcast_to(column, (feat, LANES)))[0:1]
         for layer in range(2):
             for q, cond in enumerate((plain, steered)):
                 line = 2 + 4 * step + 2 * layer + q
@@ -241,7 +247,7 @@
 
         lax.fori_loop(0, firsts // chunk, lead, 0)
 
-        count2 = 4 if seconds % 4 == 0 else (5 if seconds % 5 == 0 else 2)
+        count2 = 8 if seconds % 8 == 0 else (10 if seconds % 10 == 0 else 2)
         gain = table[2, coef_at[step]]
 
         def middle(k, carry):
@@ -282,8 +288,8 @@
         adds = table[1, coef_at[step]]
 
         def finish(row, carry):
-            total = mixed[at(row), 0:LANES] + mixed[at(row + 1), LANES : 2 * LANES]
-            total = total + mixed[at(row + 2), 2 * LANES : 3 * LANES]
+            total = jnp.where(group < LANES // 2 // chans, mixed[at(row), 0:LANES], mixed[at(row + 1), 0:LANES])
+            total = total + pltpu.roll(total, LANES // 2, 1) + mixed[at(row + 2), LANES : 2 * LANES]
             value = keeps * state[at(row + 3), :] + adds * total
             if not is_last:
                 value = jnp.where(inside(row + 3 - edge, LANES), value, 0.0)
@@ -345,12 +351,12 @@
             pltpu.VMEM((firsts, 3 * rest), jnp.float32),
             pltpu.VMEM((firsts, 3 * rest), jnp.float32),
             pltpu.VMEM((seconds, depth), jnp.bfloat16),
-            pltpu.VMEM((rows * stride, 3 * LANES), jnp.float32),
+            pltpu.VMEM((rows * stride, 2 * LANES), jnp.float32),
             pltpu.VMEM(mid_weight.shape, mid_weight.dtype),
-            pltpu.VMEM(time_embed.shape, time_embed.dtype),
+            pltpu.VMEM(time_embed.shape[::-1], time_embed.dtype),
             pltpu.VMEM((3 * depth, wide), jnp.bfloat16),
             pltpu.VMEM((depth, 3 * rest), jnp.bfloat16),
-            pltpu.VMEM((depth, 3 * LANES), jnp.bfloat16),
+            pltpu.VMEM((depth, 2 * LANES), jnp.bfloat16),
             pltpu.VMEM((up(2 + 4 * steps, 8), feat), jnp.float32),
             pltpu.VMEM((height * chans, full_cols), jnp.bfloat16),
             pltpu.VMEM((2 * margin * chans, full_cols), jnp.bfloat16),
@@ -359,16 +365,17 @@
             pltpu.VMEM(cond_embed.shape, jnp.float32),
             pltpu.VMEM((cols, LANES), jnp.float32),
             pltpu.VMEM((cols, LANES), jnp.float32),
+            pltpu.VMEM((stride, wide), jnp.int32),
             pltpu.SemaphoreType.DMA((2,)),
             pltpu.SemaphoreType.DMA((7,)),
             pltpu.SemaphoreType.DMA((7,)),
         ],
         compiler_params=pltpu.CompilerParams(
-            vmem_limit_bytes=48 * 1024 * 1024, collective_id=0, has_side_effects=True
+            vmem_limit_bytes=60 * 1024 * 1024, collective_id=0, has_side_effects=True
         ),
     )(
         time_index, coef_index, sampler_table, latents, win, mid_weight, out_weight,
-        norm_mean, norm_rstd, cond_embed, time_embed,
+        norm_mean, norm_rstd, cond_embed, time_embed.T,
     )
     return jnp.transpose(out, (1, 0, 2))
 

time: 36.1 us -> 34.8 us (0.964)
  local copies, waits for them, and re-layouts: 4.19 us -> 1.49 us
  Pallas kernels: 31.6 us -> 33.1 us
    unnamed x21 -> x0, local copies, waits for them, and re-layouts: 3.54 us -> none
    pallas_call x1, Pallas kernels: 31.6 us -> 33.1 us  [shards(): pl.pallas_call(functools.partial(section_kernel, geom), out_shape=jax.Sha...]
    transpose x1, local copies, waits for them, and re-layouts: 0.65 us -> 1.49 us  [shards(): return jnp.transpose(out, (1, 0, 2))]
where the time goes in v3:
time: 34.8 us; the launch traced here: 34.6 us
  Pallas kernels  33.1 us (95%)
  local copies, waits for them, and re-layouts  1.49 us (4%)
    pallas_call x1, Pallas kernels, shards(): pl.pallas_call(functools.partial(section_kernel, geom), out_shape=jax.Sha...  33.1 us
    transpose x1, local copies, waits for them, and re-layouts, shards(): return jnp.transpose(out, (1, 0, 2))  1.49 us

profile of v3, /device:TPU:0, one launch (start us, length us, event | category | flops | bytes accessed | tf_op | source)
XLA Modules:
  0.0 34.6 jit_solution(983225949336730955)
XLA Ops:
  0.0 33.1 %shard_map.109 = f32[8,16,128]{2,1,0:T(8,128)} custom-call(s32[2]{0:T(128)} %time_at.1, s32[2]{0:T(128)} %coef_at.1, f32[3,1000]{1,0:T(4,128)} %table.1, f32[16,8,128]{2,1,0:T(8,128)} %lat_ref.1, bf16[144,320]{1,0:T(8,128)(2,1)} %bitcast.5, bf16[3,3,320,320]{3,2,1,0:T(8,128)(2,1)} %mid_hbm.1, bf16[3,3,16,320]{3,2,1,0:T(8,128)(2,1)} %wout_ref.1, ...), custom_call_target="tpu_custom_call" | custom-call | tf_op jit(solution)/shard_map/pallas_call | solution.py:340
  33.1 1.5 %copy.12 = f32[16,8,128]{2,1,0:T(8,128)} copy(f32[16,8,128]{2,0,1:T(8,128)} %bitcast.4) | data formatting | bytes 131072 | tf_op jit(solution)/shard_map/transpose | solution.py:380

commit v4 on v3

--- a/solution.py
+++ b/solution.py
@@ -23,7 +23,7 @@
 def section_kernel(
     geom, time_at, coef_at, table, lat_ref, win_ref, mid_hbm, wout_ref, mean_ref, rstd_ref, cond_ref, time_hbm, out_ref,
     state, taps, first, lift0, lift1, thin0, thin1, low, mixed,
-    mid_ref, time_ref, wide_ref, narrow_ref, last_ref, vec_ref,
+    mid_ref, time_ref, kernel_ref, last_ref, vec_ref,
     row_send, row_recv, col_send, col_recv, cond_recv, half_send, half_recv, outside_ref,
     local_sem, send_sem, recv_sem,
 ):
@@ -130,21 +130,21 @@
     for i in range(3):
         for j in range(3):
             turned_mid = jnp.transpose(mid_ref[i, j])
-            base = i * depth
-            wide_ref[base + j * wide : base + (j + 1) * wide, :] = turned_mid[:wide, :wide]
-            narrow_ref[j * wide : (j + 1) * wide, i * rest : (i + 1) * rest] = turned_mid[:wide, wide:]
             spot = 3 * wide + j * rest
-            wide_ref[base + spot : base + spot + rest, :] = turned_mid[wide:, :wide]
-            narrow_ref[spot : spot + rest, i * rest : (i + 1) * rest] = turned_mid[wide:, wide:]
+            broad = slice(i * wide, (i + 1) * wide)
+            slim = slice(3 * wide + i * rest, 3 * wide + (i + 1) * rest)
+            kernel_ref[j * wide : (j + 1) * wide, broad] = turned_mid[:wide, :wide]
+            kernel_ref[j * wide : (j + 1) * wide, slim] = turned_mid[:wide, wide:]
+            kernel_ref[spot : spot + rest, broad] = turned_mid[wide:, :wide]
+            kernel_ref[spot : spot + rest, slim] = turned_mid[wide:, wide:]
             small = wout_ref[i, j].astype(jnp.float32)
             tall = jnp.transpose(jnp.concatenate([small] * copies, axis=0)).astype(jnp.bfloat16)
             span = slice(i * LANES // 2, (i + 1) * LANES // 2) if i < 2 else slice(LANES, 2 * LANES)
             tall = tall[:, : span.stop - span.start]
             last_ref[j * wide : (j + 1) * wide, span] = tall[:wide]
             last_ref[spot : spot + rest, span] = tall[wide:]
-        spare = 3 * wide + 3 * rest
-        wide_ref[i * depth + spare : (i + 1) * depth, :] = jnp.zeros((depth - spare, wide), jnp.bfloat16)
-    narrow_ref[spare:, :] = jnp.zeros((depth - spare, 3 * rest), jnp.bfloat16)
+    spare = 3 * feat
+    kernel_ref[spare:, :] = jnp.zeros((depth - spare, 3 * feat), jnp.bfloat16)
     last_ref[spare:, :] = jnp.zeros((depth - spare, 2 * LANES), jnp.bfloat16)
 
     cond_copy.wait()
@@ -241,26 +241,25 @@
                         parts.append(jnp.where(keep[:, : value.shape[1]], value, 0.0))
                     spread(lifts[q], row + m, *parts)
                 thins[q][at(row, chunk), :] = jnp.dot(
-                    lifts[q][at(row, chunk), :], narrow_ref[...], preferred_element_type=jnp.float32
+                    lifts[q][at(row, chunk), :], kernel_ref[...], preferred_element_type=jnp.float32
                 )
             return carry
 
         lax.fori_loop(0, firsts // chunk, lead, 0)
 
-        count2 = 8 if seconds % 8 == 0 else (10 if seconds % 10 == 0 else 2)
+        count2 = 4 if seconds % 4 == 0 else (5 if seconds % 5 == 0 else 2)
         gain = table[2, coef_at[step]]
 
         def middle(k, carry):
             row = k * count2
             found = []
             for q in range(2):
-                window = jnp.concatenate([lifts[q][at(row + tap, count2), :] for tap in range(3)], axis=1)
-                total = first[at(row + 1, count2), 0:wide] + jnp.dot(
-                    window, wide_ref[...], preferred_element_type=jnp.float32
-                )
+                total = first[at(row + 1, count2), 0:wide]
                 tail = first[at(row + 1, count2), wide:feat]
                 for tap in range(3):
-                    tail = tail + thins[q][at(row + tap, count2), tap * rest : (tap + 1) * rest]
+                    total = total + thins[q][at(row + tap, count2), tap * wide : (tap + 1) * wide]
+                    spot = 3 * wide + tap * rest
+                    tail = tail + thins[q][at(row + tap, count2), spot : spot + rest]
                 shift = vec_ref[base + 2 + q : base + 3 + q, :]
                 found.append(
                     [
@@ -348,14 +347,13 @@
             pltpu.VMEM((firsts, feat), jnp.float32),
             pltpu.VMEM((firsts, depth), jnp.bfloat16),
             pltpu.VMEM((firsts, depth), jnp.bfloat16),
-            pltpu.VMEM((firsts, 3 * rest), jnp.float32),
-            pltpu.VMEM((firsts, 3 * rest), jnp.float32),
+            pltpu.VMEM((firsts, 3 * feat), jnp.float32),
+            pltpu.VMEM((firsts, 3 * feat), jnp.float32),
             pltpu.VMEM((seconds, depth), jnp.bfloat16),
             pltpu.VMEM((rows * stride, 2 * LANES), jnp.float32),
             pltpu.VMEM(mid_weight.shape, mid_weight.dtype),
             pltpu.VMEM(time_embed.shape[::-1], time_embed.dtype),
-            pltpu.VMEM((3 * depth, wide), jnp.bfloat16),
-            pltpu.VMEM((depth, 3 * rest), jnp.bfloat16),
+            pltpu.VMEM((depth, 3 * feat), jnp.bfloat16),
             pltpu.VMEM((depth, 2 * LANES), jnp.bfloat16),
             pltpu.VMEM((up(2 + 4 * steps, 8), feat), jnp.float32),
             pltpu.VMEM((height * chans, full_cols), jnp.bfloat16),

time: 34.8 us -> 36.2 us (1.040)
  Pallas kernels: 33.1 us -> 34.5 us
    pallas_call x1, Pallas kernels: 33.1 us -> 34.5 us  [shards(): pl.pallas_call(functools.partial(section_kernel, geom), out_shape=jax.Sha...]
where the time goes in v4:
time: 36.2 us; the launch traced here: 36 us
  Pallas kernels  34.5 us (95%)
  local copies, waits for them, and re-layouts  1.49 us (4%)
    pallas_call x1, Pallas kernels, shards(): pl.pallas_call(functools.partial(section_kernel, geom), out_shape=jax.Sha...  34.5 us
    transpose x1, local copies, waits for them, and re-layouts, shards(): return jnp.transpose(out, (1, 0, 2))  1.49 us

profile of v4, /device:TPU:0, one launch (start us, length us, event | category | flops | bytes accessed | tf_op | source)
XLA Modules:
  0.0 36.0 jit_solution(16490205597511096866)
XLA Ops:
  0.0 34.5 %shard_map.109 = f32[8,16,128]{2,1,0:T(8,128)} custom-call(s32[2]{0:T(128)} %time_at.1, s32[2]{0:T(128)} %coef_at.1, f32[3,1000]{1,0:T(4,128)} %table.1, f32[16,8,128]{2,1,0:T(8,128)} %lat_ref.1, bf16[144,320]{1,0:T(8,128)(2,1)} %bitcast.5, bf16[3,3,320,320]{3,2,1,0:T(8,128)(2,1)} %mid_hbm.1, bf16[3,3,16,320]{3,2,1,0:T(8,128)(2,1)} %wout_ref.1, ...), custom_call_target="tpu_custom_call" | custom-call | tf_op jit(solution)/shard_map/pallas_call | solution.py:339
  34.5 1.5 %copy.12 = f32[16,8,128]{2,1,0:T(8,128)} copy(f32[16,8,128]{2,0,1:T(8,128)} %bitcast.4) | data formatting | bytes 131072 | tf_op jit(solution)/shard_map/transpose | solution.py:378

commit v5 on v3

--- a/solution.py
+++ b/solution.py
@@ -51,7 +51,7 @@
         return outside_ref[:, :lanes] < limit
 
     def at(row, count=1):
-        return pl.ds(pl.multiple_of(row * stride, 16), count * stride)
+        return pl.ds(row * stride if isinstance(row, int) else pl.multiple_of(row * stride, 16), count * stride)
 
     ahead = jnp.where(first_core, sub + 1, sub - 1)
     behind = jnp.where(first_core, sub - 1, sub + 1)
@@ -86,13 +86,6 @@
 
     def stand(block):
         return jnp.transpose(jnp.concatenate([block] * copies, axis=0))
-
-    bodies = [stand(lat_ref[:, y, :]) for y in range(height)]
-    for y in range(0, height, 2):
-        pair = [
-            jnp.where(first_core, bodies[y + k][full_cols - side :], bodies[y + k][:side]) for k in range(2)
-        ]
-        col_send[y * side : (y + 2) * side, :] = jnp.concatenate(pair, axis=0).astype(jnp.bfloat16)
 
     def count(flag):
         return flag.astype(jnp.int32)
@@ -121,10 +114,20 @@
         (goes & has_down, comes & has_up, remote(3, col_send.at[col_all - col_part : col_all], col_recv.at[0:col_part], {"band": band + 1, "sub": ahead})),
         (goes & has_up, comes & has_down, remote(4, col_send.at[0:col_part], col_recv.at[col_part + col_all : 2 * col_part + col_all], {"band": band - 1, "sub": ahead})),
     ]
-    for go, come, copy in sends:
+    for go, come, copy in sends[:2]:
         pl.when(go)(copy.start)
     cond_copy = remote(5, cond_ref, cond_recv, partner)
     cond_copy.start()
+
+    bodies = [stand(lat_ref[:, y, :]) for y in range(height)]
+    for y in range(0, height, 2):
+        pair = [
+            jnp.where(first_core, bodies[y + k][full_cols - side :], bodies[y + k][:side]) for k in range(2)
+        ]
+        col_send[y * side : (y + 2) * side, :] = jnp.concatenate(pair, axis=0).astype(jnp.bfloat16)
+
+    for go, come, copy in sends[2:]:
+        pl.when(go)(copy.start)
 
     mid_copy.wait()
     for i in range(3):
@@ -215,7 +218,7 @@
             mixed[at(row), LANES : 2 * LANES] = after
             return carry
 
-        lax.fori_loop(0, now_rows, lay, 0)
+        lax.fori_loop(0, now_rows, lay, 0, unroll=True)
 
         chunk = 6 if firsts % 6 == 0 else 2
 
@@ -245,7 +248,7 @@
                 )
             return carry
 
-        lax.fori_loop(0, firsts // chunk, lead, 0)
+        lax.fori_loop(0, firsts // chunk, lead, 0, unroll=True)
 
         count2 = 8 if seconds % 8 == 0 else (10 if seconds % 10 == 0 else 2)
         gain = table[2, coef_at[step]]
@@ -282,7 +285,7 @@
             mixed[at(row, count2), :] = jnp.dot(low[at(row, count2), :], last_ref[...], preferred_element_type=jnp.float32)
             return carry
 
-        lax.fori_loop(0, seconds // count2, middle, 0)
+        lax.fori_loop(0, seconds // count2, middle, 0, unroll=True)
 
         keeps = table[0, coef_at[step]]
         adds = table[1, coef_at[step]]
@@ -296,7 +299,7 @@
             state[at(row), :] = value
             return carry
 
-        lax.fori_loop(0, now_rows - 6, finish, 0)
+        lax.fori_loop(0, now_rows - 6, finish, 0, unroll=True)
 
     group = lax.broadcasted_iota(jnp.int32, (cols, LANES), 1) // chans
     packed = state[side : side + cols, :]

time: 34.8 us -> 28.5 us (0.82)
  Pallas kernels: 33.1 us -> 26.8 us
    pallas_call x1, Pallas kernels: 33.1 us -> 26.8 us  [shards(): pl.pallas_call(functools.partial(section_kernel, geom), out_shape=jax.Sha...]
where the time goes in v5:
time: 28.5 us; the launch traced here: 28.3 us
  Pallas kernels  26.8 us (94%)
  local copies, waits for them, and re-layouts  1.49 us (5%)
    pallas_call x1, Pallas kernels, shards(): pl.pallas_call(functools.partial(section_kernel, geom), out_shape=jax.Sha...  26.8 us
    transpose x1, local copies, waits for them, and re-layouts, shards(): return jnp.transpose(out, (1, 0, 2))  1.49 us

profile of v5, /device:TPU:0, one launch (start us, length us, event | category | flops | bytes accessed | tf_op | source)
XLA Modules:
  0.0 28.3 jit_solution(15546264613868685790)
XLA Ops:
  0.0 26.8 %shard_map.109 = f32[8,16,128]{2,1,0:T(8,128)} custom-call(s32[2]{0:T(128)} %time_at.1, s32[2]{0:T(128)} %coef_at.1, f32[3,1000]{1,0:T(4,128)} %table.1, f32[16,8,128]{2,1,0:T(8,128)} %lat_ref.1, bf16[144,320]{1,0:T(8,128)(2,1)} %bitcast.5, bf16[3,3,320,320]{3,2,1,0:T(8,128)(2,1)} %mid_hbm.1, bf16[3,3,16,320]{3,2,1,0:T(8,128)(2,1)} %wout_ref.1, ...), custom_call_target="tpu_custom_call" | custom-call | tf_op jit(solution)/shard_map/pallas_call | solution.py:343
  26.8 1.5 %copy.12 = f32[16,8,128]{2,1,0:T(8,128)} copy(f32[16,8,128]{2,0,1:T(8,128)} %bitcast.4) | data formatting | bytes 131072 | tf_op jit(solution)/shard_map/transpose | solution.py:383

commit v6 on v5

--- a/solution.py
+++ b/solution.py
@@ -22,7 +22,7 @@
 
 def section_kernel(
     geom, time_at, coef_at, table, lat_ref, win_ref, mid_hbm, wout_ref, mean_ref, rstd_ref, cond_ref, time_hbm, out_ref,
-    state, taps, first, lift0, lift1, thin0, thin1, low, mixed,
+    state, taps, first, lift0, lift1, thin0, thin1, low, mixed, noise,
     mid_ref, time_ref, wide_ref, narrow_ref, last_ref, vec_ref,
     row_send, row_recv, col_send, col_recv, cond_recv, half_send, half_recv, outside_ref,
     local_sem, send_sem, recv_sem,
@@ -229,9 +229,9 @@
                 two = mixed[at(row + m + 1), 0:LANES]
                 three = mixed[at(row + m + 2), 0:LANES]
                 body = jnp.where(group < 3, one, jnp.where(group < 6, two, three))
-                taps[at(m), 0:LANES] = body.astype(jnp.bfloat16)
-                taps[at(m), LANES : LANES + chans] = mixed[at(row + m + 2), LANES : LANES + chans].astype(jnp.bfloat16)
-            field = jnp.dot(taps[...][: chunk * stride], win_ref[...], preferred_element_type=jnp.float32)
+                taps[at(row + m), 0:LANES] = body.astype(jnp.bfloat16)
+                taps[at(row + m), LANES : LANES + chans] = mixed[at(row + m + 2), LANES : LANES + chans].astype(jnp.bfloat16)
+            field = jnp.dot(taps[at(row, chunk), :], win_ref[...], preferred_element_type=jnp.float32)
             first[at(row, chunk), :] = field
             for q in range(2):
                 shift = vec_ref[base + q : base + q + 1, :]
@@ -250,7 +250,7 @@
 
         lax.fori_loop(0, firsts // chunk, lead, 0, unroll=True)
 
-        count2 = 8 if seconds % 8 == 0 else (10 if seconds % 10 == 0 else 2)
+        count2 = 8 if seconds % 8 == 0 else (5 if seconds % 5 == 0 else 2)
         gain = table[2, coef_at[step]]
 
         def middle(k, carry):
@@ -282,7 +282,7 @@
                         for part in lowered
                     ],
                 )
-            mixed[at(row, count2), :] = jnp.dot(low[at(row, count2), :], last_ref[...], preferred_element_type=jnp.float32)
+            noise[at(row, count2), :] = jnp.dot(low[at(row, count2), :], last_ref[...], preferred_element_type=jnp.float32)
             return carry
 
         lax.fori_loop(0, seconds // count2, middle, 0, unroll=True)
@@ -291,8 +291,8 @@
         adds = table[1, coef_at[step]]
 
         def finish(row, carry):
-            total = jnp.where(group < LANES // 2 // chans, mixed[at(row), 0:LANES], mixed[at(row + 1), 0:LANES])
-            total = total + pltpu.roll(total, LANES // 2, 1) + mixed[at(row + 2), LANES : 2 * LANES]
+            total = jnp.where(group < LANES // 2 // chans, noise[at(row), 0:LANES], noise[at(row + 1), 0:LANES])
+            total = total + pltpu.roll(total, LANES // 2, 1) + noise[at(row + 2), LANES : 2 * LANES]
             value = keeps * state[at(row + 3), :] + adds * total
             if not is_last:
                 value = jnp.where(inside(row + 3 - edge, LANES), value, 0.0)
@@ -347,7 +347,7 @@
         out_specs=whole,
         scratch_shapes=[
             pltpu.VMEM((rows * stride, LANES), jnp.float32),
-            pltpu.VMEM((6 * stride, 9 * chans), jnp.bfloat16),
+            pltpu.VMEM((firsts, 9 * chans), jnp.bfloat16),
             pltpu.VMEM((firsts, feat), jnp.float32),
             pltpu.VMEM((firsts, depth), jnp.bfloat16),
             pltpu.VMEM((firsts, depth), jnp.bfloat16),
@@ -355,6 +355,7 @@
             pltpu.VMEM((firsts, 3 * rest), jnp.float32),
             pltpu.VMEM((seconds, depth), jnp.bfloat16),
             pltpu.VMEM((rows * stride, 2 * LANES), jnp.float32),
+            pltpu.VMEM((seconds, 2 * LANES), jnp.float32),
             pltpu.VMEM(mid_weight.shape, mid_weight.dtype),
             pltpu.VMEM(time_embed.shape[::-1], time_embed.dtype),
             pltpu.VMEM((3 * depth, wide), jnp.bfloat16),
@@ -374,7 +375,7 @@
             pltpu.SemaphoreType.DMA((7,)),
         ],
         compiler_params=pltpu.CompilerParams(
-            vmem_limit_bytes=60 * 1024 * 1024, collective_id=0, has_side_effects=True
+            vmem_limit_bytes=54 * 1024 * 1024, collective_id=0, has_side_effects=True
         ),
     )(
         time_index, coef_index, sampler_table, latents, win, mid_weight, out_weight,

time: 28.5 us -> 28.2 us (0.989)
  Pallas kernels: 26.8 us -> 26.5 us
where the time goes in v6:
time: 28.2 us; the launch traced here: 28 us
  Pallas kernels  26.5 us (94%)
  local copies, waits for them, and re-layouts  1.49 us (5%)
    pallas_call x1, Pallas kernels, shards(): pl.pallas_call(functools.partial(section_kernel, geom), out_shape=jax.Sha...  26.5 us
    transpose x1, local copies, waits for them, and re-layouts, shards(): return jnp.transpose(out, (1, 0, 2))  1.49 us

profile of v6, /device:TPU:0, one launch (start us, length us, event | category | flops | bytes accessed | tf_op | source)
XLA Modules:
  0.0 28.0 jit_solution(8298095230660550076)
XLA Ops:
  0.0 26.5 %shard_map.109 = f32[8,16,128]{2,1,0:T(8,128)} custom-call(s32[2]{0:T(128)} %time_at.1, s32[2]{0:T(128)} %coef_at.1, f32[3,1000]{1,0:T(4,128)} %table.1, f32[16,8,128]{2,1,0:T(8,128)} %lat_ref.1, bf16[144,320]{1,0:T(8,128)(2,1)} %bitcast.5, bf16[3,3,320,320]{3,2,1,0:T(8,128)(2,1)} %mid_hbm.1, bf16[3,3,16,320]{3,2,1,0:T(8,128)(2,1)} %wout_ref.1, ...), custom_call_target="tpu_custom_call" | custom-call | tf_op jit(solution)/shard_map/pallas_call | solution.py:343
  26.5 1.5 %copy.12 = f32[16,8,128]{2,1,0:T(8,128)} copy(f32[16,8,128]{2,0,1:T(8,128)} %bitcast.4) | data formatting | bytes 131072 | tf_op jit(solution)/shard_map/transpose | solution.py:384

commit v7 on v6

--- a/solution.py
+++ b/solution.py
@@ -250,7 +250,7 @@
 
         lax.fori_loop(0, firsts // chunk, lead, 0, unroll=True)
 
-        count2 = 8 if seconds % 8 == 0 else (5 if seconds % 5 == 0 else 2)
+        count2 = 4 if seconds % 4 == 0 else (5 if seconds % 5 == 0 else 2)
         gain = table[2, coef_at[step]]
 
         def middle(k, carry):
@@ -375,7 +375,7 @@
             pltpu.SemaphoreType.DMA((7,)),
         ],
         compiler_params=pltpu.CompilerParams(
-            vmem_limit_bytes=54 * 1024 * 1024, collective_id=0, has_side_effects=True
+            vmem_limit_bytes=52 * 1024 * 1024, collective_id=0, has_side_effects=True
         ),
     )(
         time_index, coef_index, sampler_table, latents, win, mid_weight, out_weight,

time: 28.2 us -> 34.9 us (1.24)
  local copies, waits for them, and re-layouts: 1.49 us -> 8.67 us
  Pallas kernels: 26.5 us -> 25.9 us
    unnamed x0 -> x20, local copies, waits for them, and re-layouts: none -> 8.02 us
    transpose x1, local copies, waits for them, and re-layouts: 1.49 us -> 0.65 us  [shards(): return jnp.transpose(out, (1, 0, 2))]
    pallas_call x1, Pallas kernels: 26.5 us -> 25.9 us  [shards(): pl.pallas_call(functools.partial(section_kernel, geom), out_shape=jax.Sha...]
where the time goes in v7:
time: 34.9 us; the launch traced here: 34.5 us
  Pallas kernels  25.9 us (74%)
  local copies, waits for them, and re-layouts  8.67 us (25%)
    pallas_call x1, Pallas kernels, shards(): pl.pallas_call(functools.partial(section_kernel, geom), out_shape=jax.Sha...  25.9 us
    unnamed x20, local copies, waits for them, and re-layouts  8.02 us

profile of v7, /device:TPU:0, one launch (start us, length us, event | category | flops | bytes accessed | tf_op | source)
XLA Modules:
  0.0 34.5 jit_solution(8996099339487742689)
XLA Ops:
  0.0 0.0 copy-start
  0.0 1.3 %copy-done = f32[1000,320]{0,1:T(8,128)S(1)} copy-done((f32[1000,320]{0,1:T(8,128)S(1)}, f32[1000,320]{0,1:T(8,128)}, u32[]{:S(2)}) %copy-start) | copy-done | bytes 1280024
  1.3 0.0 copy-start.1
  1.3 0.9 %copy-done.1 = bf16[3,3,16,320]{3,2,1,0:T(8,128)(2,1)S(1)} copy-done((bf16[3,3,16,320]{3,2,1,0:T(8,128)(2,1)S(1)}, bf16[3,3,16,320]{3,2,1,0:T(8,128)(2,1)}, u32[]{:S(2)}) %copy-start.1) | copy-done | bytes 92184
  2.2 0.0 copy-start.2
  2.2 0.9 %copy-done.2 = bf16[3,3,16,320]{3,2,1,0:T(8,128)(2,1)S(1)} copy-done((bf16[3,3,16,320]{3,2,1,0:T(8,128)(2,1)S(1)}, bf16[3,3,16,320]{3,2,1,0:T(8,128)(2,1)}, u32[]{:S(2)}) %copy-start.2) | copy-done | bytes 92184
  3.1 0.0 copy-start.3
  3.1 0.8 %copy-done.3 = f32[16,8,128]{2,1,0:T(8,128)S(1)} copy-done((f32[16,8,128]{2,1,0:T(8,128)S(1)}, f32[16,8,128]{2,1,0:T(8,128)}, u32[]{:S(2)}) %copy-start.3) | copy-done | bytes 65560
  4.0 0.0 copy-start.4
  4.0 0.7 %copy-done.4 = f32[3,1000]{1,0:T(4,128)S(1)} copy-done((f32[3,1000]{1,0:T(4,128)S(1)}, f32[3,1000]{1,0:T(4,128)}, u32[]{:S(2)}) %copy-start.4) | copy-done | bytes 12024
  4.7 0.0 copy-start.5
  4.7 0.7 %copy-done.5 = f32[2,320]{1,0:T(2,128)S(1)} copy-done((f32[2,320]{1,0:T(2,128)S(1)}, f32[2,320]{1,0:T(2,128)}, u32[]{:S(2)}) %copy-start.5) | copy-done | bytes 2584
  5.4 0.0 copy-start.6
  5.4 0.7 %copy-done.6 = f32[2,320]{1,0:T(2,128)S(1)} copy-done((f32[2,320]{1,0:T(2,128)S(1)}, f32[2,320]{1,0:T(2,128)}, u32[]{:S(2)}) %copy-start.6) | copy-done | bytes 2584
  6.0 0.0 copy-start.7
  6.0 0.7 %copy-done.7 = f32[1,320]{1,0:T(1,128)S(1)} copy-done((f32[1,320]{1,0:T(1,128)S(1)}, f32[1,320]{1,0:T(1,128)}, u32[]{:S(2)}) %copy-start.7) | copy-done | bytes 1304
  6.7 0.0 copy-start.8
  6.7 0.7 %copy-done.8 = s32[2]{0:T(128)S(1)} copy-done((s32[2]{0:T(128)S(1)}, s32[2]{0:T(128)}, u32[]{:S(2)}) %copy-start.8) | copy-done | bytes 32
  7.4 0.0 copy-start.9
  7.4 0.7 %copy-done.9 = s32[2]{0:T(128)S(1)} copy-done((s32[2]{0:T(128)S(1)}, s32[2]{0:T(128)}, u32[]{:S(2)}) %copy-start.9) | copy-done | bytes 32
  8.0 25.9 %shard_map.109 = f32[8,16,128]{2,1,0:T(8,128)S(1)} custom-call(s32[2]{0:T(128)S(1)} %copy-done.8, s32[2]{0:T(128)S(1)} %copy-done.9, f32[3,1000]{1,0:T(4,128)S(1)} %copy-done.4, f32[16,8,128]{2,1,0:T(8,128)S(1)} %copy-done.3, bf16[144,320]{1,0:T(8,128)(2,1)S(1)} %bitcast.5, bf16[3,3,320,320]{3,2,1,0:T(8,128)(2,1)} %mid_hbm.1, ...), custom_call_target="tpu_custom_call" | custom-call | tf_op jit(solution)/shard_map/pallas_call | solution.py:343
  33.9 0.7 %copy.12 = f32[16,8,128]{2,1,0:T(8,128)} copy(f32[16,8,128]{2,0,1:T(8,128)S(1)} %bitcast.4) | data formatting | bytes 131072 | tf_op jit(solution)/shard_map/transpose | solution.py:384
Async XLA Ops:
  0.0 1.3 %copy-start = (f32[1000,320]{0,1:T(8,128)S(1)}, f32[1000,320]{0,1:T(8,128)}, u32[]{:S(2)}) copy-start(f32[1000,320]{0,1:T(8,128)} %param.18) | copy-start | bytes 3840004
  1.3 0.9 %copy-start.1 = (bf16[3,3,16,320]{3,2,1,0:T(8,128)(2,1)S(1)}, bf16[3,3,16,320]{3,2,1,0:T(8,128)(2,1)}, u32[]{:S(2)}) copy-start(bf16[3,3,16,320]{3,2,1,0:T(8,128)(2,1)} %param.12) | copy-start | bytes 276484
  2.2 0.9 %copy-start.2 = (bf16[3,3,16,320]{3,2,1,0:T(8,128)(2,1)S(1)}, bf16[3,3,16,320]{3,2,1,0:T(8,128)(2,1)}, u32[]{:S(2)}) copy-start(bf16[3,3,16,320]{3,2,1,0:T(8,128)(2,1)} %wout_ref.1) | copy-start | bytes 276484
  3.1 0.8 %copy-start.3 = (f32[16,8,128]{2,1,0:T(8,128)S(1)}, f32[16,8,128]{2,1,0:T(8,128)}, u32[]{:S(2)}) copy-start(f32[16,8,128]{2,1,0:T(8,128)} %lat_ref.1) | copy-start | bytes 196612
  4.0 0.7 %copy-start.4 = (f32[3,1000]{1,0:T(4,128)S(1)}, f32[3,1000]{1,0:T(4,128)}, u32[]{:S(2)}) copy-start(f32[3,1000]{1,0:T(4,128)} %table.1) | copy-start | bytes 36004
  4.7 0.7 %copy-start.5 = (f32[2,320]{1,0:T(2,128)S(1)}, f32[2,320]{1,0:T(2,128)}, u32[]{:S(2)}) copy-start(f32[2,320]{1,0:T(2,128)} %mean_ref.1) | copy-start | bytes 7684
  5.4 0.7 %copy-start.6 = (f32[2,320]{1,0:T(2,128)S(1)}, f32[2,320]{1,0:T(2,128)}, u32[]{:S(2)}) copy-start(f32[2,320]{1,0:T(2,128)} %rstd_ref.1) | copy-start | bytes 7684
  6.0 0.7 %copy-start.7 = (f32[1,320]{1,0:T(1,128)S(1)}, f32[1,320]{1,0:T(1,128)}, u32[]{:S(2)}) copy-start(f32[1,320]{1,0:T(1,128)} %cond_ref.1) | copy-start | bytes 3844
  6.7 0.7 %copy-start.8 = (s32[2]{0:T(128)S(1)}, s32[2]{0:T(128)}, u32[]{:S(2)}) copy-start(s32[2]{0:T(128)} %time_at.1) | copy-start | bytes 28
  7.4 0.7 %copy-start.9 = (s32[2]{0:T(128)S(1)}, s32[2]{0:T(128)}, u32[]{:S(2)}) copy-start(s32[2]{0:T(128)} %coef_at.1) | copy-start | bytes 28
